TPU v7x, 512 devices: a whole 4x4x16 slice. The times are simulated.
512 devices in a mesh: dp: 64 (over z, y), tensor: 8 (over x, core).
Axes of the slice: x: 4, y: 4, z: 16, core: 2. Of those that a mesh axis runs over, the one named last changes fastest.
Arguments:
- patches: bfloat16 [2048, 8, 3072], P('dp', None, 'tensor'), may hold values from -10 to 10
- counts: int32 [2048], P('dp'), may hold values from 1 to 8, as said below
- target: int32 [2048], P('dp'), may hold values from 0 to 63, as said below
- ln_gain: float32 [3072], replicated, may hold values from 0.25 to 1.75
- w_qkv: bfloat16 [3, 3072, 3072], P(None, 'dp', 'tensor'), may hold values from -1 to 1
- w_out: bfloat16 [3072, 3072], P('tensor', 'dp'), may hold values from -0.109375 to 0.109375
- cotangent: bfloat16 [2048, 8, 3072], P('dp', None, 'tensor'), may hold values from -6 to 6
Outputs:
- mixed: bfloat16 [2048, 8, 3072], P('dp', None, 'tensor')
- patch_grad: bfloat16 [2048, 8, 3072], P('dp', None, 'tensor')
Inputs may be any that keep to these rules, and one draw needn't show every extreme that they name: `counts`: every draw has an image of 8 live patches and one of a single live patch. `target`: the 32 images of one source device go to 32 different devices, and every device receives exactly one image of each slot k.
All inputs are finite; a program needn't handle non-finite values.
Results may differ from a plain program's by a relative error of at most 0.014.
Values may be sent and summed in bfloat16 or wider, within the bound.
A program may use at most 64 MiB of HBM per device.

v0:
```python
import jax
import jax.numpy as jnp
from jax import lax
from jax.sharding import PartitionSpec as P

HD = 128


def normalize(rows):
    row_mean = jnp.mean(rows, axis=-1, keepdims=True)
    centred = rows - row_mean
    inv_std = lax.rsqrt(jnp.mean(centred * centred, axis=-1, keepdims=True) + 1e-06)
    return (centred * inv_std, inv_std)


def right_dot(left, weight):
    return lax.dot_general(
        left, weight, (((1,), (1,)), ((), ())), preferred_element_type=jnp.float32
    )


def per_device(patches, counts, target, ln_gain, w_qkv, w_out, cotangent):
    peer_count = lax.axis_size("dp")
    image_count, slot_len, width_loc = patches.shape
    total = image_count * slot_len
    heads_loc = w_out.shape[0] // HD
    score_scale = HD ** (-0.5)
    proj_full, out_full = (
        lax.all_gather(w_qkv, "dp", axis=1, tiled=True),
        lax.all_gather(w_out, "dp", axis=1, tiled=True),
    )
    slot_ids = jnp.arange(image_count, dtype=jnp.int32)
    to_peer = target[None, :] == jnp.arange(peer_count, dtype=jnp.int32)[:, None]
    send = jnp.einsum(
        "pi,isd->psd", to_peer.astype(jnp.bfloat16), patches, preferred_element_type=jnp.float32
    ).astype(jnp.bfloat16)
    send_count = jnp.sum(jnp.where(to_peer, counts[None, :], 0), axis=1)
    send_slot = jnp.sum(jnp.where(to_peer, slot_ids[None, :], 0), axis=1) + jnp.where(
        jnp.any(to_peer, axis=1), 0, -1
    )
    meta = jnp.stack([send_count, send_slot], axis=1)
    received, meta_in = (
        lax.all_to_all(send, "dp", split_axis=0, concat_axis=0, tiled=True),
        lax.all_to_all(meta, "dp", split_axis=0, concat_axis=0, tiled=True),
    )
    pick = (meta_in[None, :, 1] == slot_ids[:, None]) & (meta_in[None, :, 0] > 0)
    local = jnp.einsum(
        "ip,psd->isd", pick.astype(jnp.bfloat16), received, preferred_element_type=jnp.float32
    ).astype(jnp.bfloat16)
    local_counts = jnp.sum(jnp.where(pick, meta_in[None, :, 0], 0), axis=1)
    positions = jnp.arange(slot_len, dtype=jnp.int32)
    key_ok = positions[None, :] < local_counts[:, None]
    row_ok = key_ok.reshape(total, 1)
    local_rows = local.reshape(total, width_loc)
    gathered = lax.all_gather(local_rows, "tensor", axis=1, tiled=True)
    unit_rows, inv_std = normalize(gathered.astype(jnp.float32))
    normed = (unit_rows * ln_gain).astype(jnp.bfloat16)
    shape4 = (image_count, slot_len, heads_loc, HD)
    query = (
        jnp.dot(normed, proj_full[0], preferred_element_type=jnp.float32)
        .astype(jnp.bfloat16)
        .reshape(shape4)
    )
    keys = (
        jnp.dot(normed, proj_full[1], preferred_element_type=jnp.float32)
        .astype(jnp.bfloat16)
        .reshape(shape4)
    )
    values = (
        jnp.dot(normed, proj_full[2], preferred_element_type=jnp.float32)
        .astype(jnp.bfloat16)
        .reshape(shape4)
    )
    scores = (
        jnp.einsum("ishd,ithd->ihst", query, keys, preferred_element_type=jnp.float32) * score_scale
    )
    scores = jnp.where(key_ok[:, None, None, :], scores, -1e30)
    top = jnp.max(scores, axis=-1, keepdims=True)
    expo = jnp.exp(scores - top)
    probs = (expo / jnp.sum(expo, axis=-1, keepdims=True)).astype(jnp.bfloat16)
    attn = jnp.einsum("ihst,ithd->ishd", probs, values, preferred_element_type=jnp.float32).astype(
        jnp.bfloat16
    )
    branch_part = jnp.dot(
        attn.reshape(total, heads_loc * HD), out_full, preferred_element_type=jnp.float32
    )
    branch = lax.psum_scatter(
        branch_part.astype(jnp.bfloat16), "tensor", scatter_dimension=1, tiled=True
    ).astype(jnp.float32)
    mixed = jnp.where(row_ok, local_rows.astype(jnp.float32) + branch, 0.0).astype(jnp.bfloat16)
    grad_rows = jnp.where(row_ok, cotangent.reshape(total, width_loc), jnp.zeros((), jnp.bfloat16))
    grad_full = lax.all_gather(grad_rows, "tensor", axis=1, tiled=True)
    attn_grad = right_dot(grad_full, out_full).astype(jnp.bfloat16).reshape(shape4)
    dprobs = jnp.einsum("ishd,ithd->ihst", attn_grad, values, preferred_element_type=jnp.float32)
    value_grad = jnp.einsum(
        "ihst,ishd->ithd", probs, attn_grad, preferred_element_type=jnp.float32
    ).astype(jnp.bfloat16)
    probs32 = probs.astype(jnp.float32)
    inner = jnp.sum(dprobs * probs32, axis=-1, keepdims=True)
    score_grad = (probs32 * (dprobs - inner) * score_scale).astype(jnp.bfloat16)
    query_grad = jnp.einsum(
        "ihst,ithd->ishd", score_grad, keys, preferred_element_type=jnp.float32
    ).astype(jnp.bfloat16)
    key_grad = jnp.einsum(
        "ihst,ishd->ithd", score_grad, query, preferred_element_type=jnp.float32
    ).astype(jnp.bfloat16)
    flat = (total, heads_loc * HD)
    normed_part = right_dot(query_grad.reshape(flat), proj_full[0])
    normed_part = normed_part + right_dot(key_grad.reshape(flat), proj_full[1])
    normed_part = normed_part + right_dot(value_grad.reshape(flat), proj_full[2])
    start = lax.axis_index("tensor") * width_loc
    normed_grad = lax.psum(normed_part.astype(jnp.bfloat16), "tensor").astype(jnp.float32)
    scaled = normed_grad * ln_gain
    back_full = inv_std * (
        scaled
        - jnp.mean(scaled, axis=-1, keepdims=True)
        - unit_rows * jnp.mean(scaled * unit_rows, axis=-1, keepdims=True)
    )
    norm_back = lax.dynamic_slice_in_dim(back_full, start, width_loc, 1)
    moved_grad = jnp.where(row_ok, grad_rows.astype(jnp.float32) + norm_back, 0.0).astype(
        jnp.bfloat16
    )
    returning = jnp.einsum(
        "ip,isd->psd",
        pick.astype(jnp.bfloat16),
        moved_grad.reshape(image_count, slot_len, width_loc),
        preferred_element_type=jnp.float32,
    ).astype(jnp.bfloat16)
    arrived = lax.all_to_all(returning, "dp", split_axis=0, concat_axis=0, tiled=True)
    patch_grad = jnp.einsum(
        "pi,psd->isd", to_peer.astype(jnp.bfloat16), arrived, preferred_element_type=jnp.float32
    ).astype(jnp.bfloat16)
    return (mixed.reshape(image_count, slot_len, width_loc), patch_grad)


def solution(mesh):
    in_specs = (
        P("dp", None, "tensor"),
        P("dp"),
        P("dp"),
        P(),
        P(None, "dp", "tensor"),
        P("tensor", "dp"),
        P("dp", None, "tensor"),
    )
    out_specs = (P("dp", None, "tensor"), P("dp", None, "tensor"))
    return jax.shard_map(
        per_device, mesh=mesh, in_specs=in_specs, out_specs=out_specs, check_vma=False
    )
```

profile of v0, /device:TPU:1, one launch (start us, length us, event | category | flops | bytes accessed | tf_op | source)
XLA Modules:
  0.0 617.9 jit_solution(11431145788605447965)
XLA Ops:
  7.2 0.8 fusion.51
  8.0 0.8 select_reduce_fusion.2
  8.8 0.7 copy.16
  9.5 19.3 %all-to-all-start = ((s32[64,1,2]{2,1,0:T(1,128)}), s32[64,1,2]{2,1,0:T(1,128)S(1)}, u32[]{:S(2)}, u32[]{:S(2)}) async-start(s32[64,1,2]{2,1,0:T(1,128)} %copy.16), calls=%async_computation | async-start | bytes 65536 | tf_op jit(solution)/shard_map/all_to_all | solution.py:44
  28.8 1.0 convolution_convert_fusion.2
  29.8 1.0 copy.19
  30.8 11.3 %all-to-all-done = s32[64,1,2]{2,1,0:T(1,128)S(1)} async-done(((s32[64,1,2]{2,1,0:T(1,128)}), s32[64,1,2]{2,1,0:T(1,128)S(1)}, u32[]{:S(2)}, u32[]{:S(2)}) %all-to-all-start) | async-done | bytes 544 | tf_op jit(solution)/shard_map/all_to_all | solution.py:44
  42.1 4.6 all-to-all-start.1
  46.9 23.2 %all-to-all-done.1 = bf16[64,8,384]{2,1,0:T(8,128)(2,1)S(1)} async-done(((bf16[64,8,384]{2,1,0:T(8,128)(2,1)}), bf16[64,8,384]{2,1,0:T(8,128)(2,1)S(1)}, u32[]{:S(2)}, u32[]{:S(2)}) %all-to-all-start.1) | async-done | bytes 393248 | tf_op jit(solution)/shard_map/all_to_all | solution.py:43
  70.1 0.2 convolution_convert_fusion.9
  70.4 0.7 copy.43
  71.2 0.1 select_reduce_fusion
  71.3 0.1 iota_compare_fusion.2
  71.4 0.1 lt.30
  71.5 0.8 bitcast_select_fusion
  72.3 0.7 all-gather.9.cloned.1.call-update
  73.1 0.5 all-gather.7.cloned.1.call-update
  73.7 26.0 %all-gather.5.cloned.1.call-done = bf16[256,3072]{1,0:T(8,128)(2,1)} async-done(((bf16[256,384]{1,0:T(8,128)(2,1)}), bf16[256,3072]{1,0:T(8,128)(2,1)}) %all-gather.5.cloned.1.call-update) | async-done | bytes 1572880 | tf_op jit(solution)/shard_map/all_gather | solution.py:55
  99.7 1.7 convert_reduce_fusion
  101.4 2.1 fusion.5
  103.5 31.2 %all-gather.11.cloned.1.call-done = bf16[256,3072]{1,0:T(8,128)(2,1)} async-done(((bf16[256,384]{1,0:T(8,128)(2,1)}), bf16[256,3072]{1,0:T(8,128)(2,1)}) %all-gather.11.cloned.1.call-update) | async-done | bytes 1572880 | tf_op jit(solution)/shard_map/all_gather | solution.py:92
  134.8 136.1 %all-gather.9.cloned.1.call-done = bf16[384,3072]{0,1:T(8,128)(2,1)} async-done(((bf16[384,48]{0,1:T(8,128)(2,1)}), bf16[384,3072]{0,1:T(8,128)(2,1)}) %all-gather.9.cloned.1.call-update) | async-done | bytes 2359312 | tf_op jit(solution)/shard_map/all_gather | solution.py:30
  270.9 3.1 fusion.25
  274.0 150.4 %all-gather.7.cloned.1.call-done = bf16[3,3072,384]{2,1,0:T(8,128)(2,1)} async-done(((bf16[3,48,384]{2,1,0:T(8,128)(2,1)}), bf16[3,3072,384]{2,1,0:T(8,128)(2,1)}) %all-gather.7.cloned.1.call-update) | async-done | bytes 7077904 | tf_op jit(solution)/shard_map/all_gather | solution.py:29
  424.4 2.9 fusion.26
  427.3 0.2 fusion.69
  427.5 0.6 copy-done.2
  428.1 1.1 fusion.28
  429.2 1.8 fusion.27
  431.0 1.4 fusion.68
  432.5 1.3 fusion.23
  433.8 0.4 fusion.22
  434.1 2.7 fusion.7
  436.8 4.4 convolution_add_fusion.1
  441.3 5.0 fusion.2
  446.3 0.2 reduce-scatter.4.cloned.1.call-start
  446.5 3.1 convolution_convert_fusion
  449.6 1.7 copy.30
  451.3 75.1 %all-reduce.2.cloned.1.call-done = bf16[256,3072]{1,0:T(8,128)(2,1)} async-done(((bf16[256,3072]{1,0:T(8,128)(2,1)}), bf16[256,3072]{1,0:T(8,128)(2,1)}) %all-reduce.2.cloned.1.call-update) | async-done | bytes 1572880 | tf_op jit(solution)/shard_map/psum | solution.py:112
  526.4 4.9 fusion.16
  531.3 37.6 %reduce-scatter.4.cloned.1.call-done = bf16[384,256]{1,0:T(8,128)(2,1)} async-done(((bf16[3072,256]{1,0:T(8,128)(2,1)}), bf16[384,256]{1,0:T(8,128)(2,1)}) %reduce-scatter.4.cloned.1.call-update) | async-done | bytes 196624
  568.9 1.1 copy.31
  570.0 2.0 fusion.45
  572.1 0.3 convolution_convert_fusion.1
  572.4 0.2 copy.25
  572.6 37.4 %all_to_all.22 = bf16[64,8,384]{2,1,0:T(8,128)(2,1)S(1)} all-to-all(bf16[64,8,384]{2,1,0:T(8,128)(2,1)S(1)} %copy.25), channel_id=1, replica_groups=mesh['dp'=64,'tensor'=8] {'dp'}, dimensions={0} | all-to-all | bytes 786432 | tf_op jit(solution)/shard_map/all_to_all | solution.py:129
  610.0 0.3 convolution_convert_fusion.4
  610.3 0.7 copy.27
  (49 shorter events, 0.5 us)
Async XLA Ops:
  7.2 21.6 %copy-start = (bf16[32,8,384]{2,1,0:T(8,128)(2,1)S(1)}, bf16[32,8,384]{2,1,0:T(8,128)(2,1)}, u32[]{:S(2)}) copy-start(bf16[32,8,384]{2,1,0:T(8,128)(2,1)} %param.7) | copy-start | bytes 589828
  7.2 64.3 %copy-start.5 = (bf16[32,8,384]{2,1,0:T(8,128)(2,1)S(1)}, bf16[32,8,384]{2,1,0:T(8,128)(2,1)}, u32[]{:S(2)}) copy-start(bf16[32,8,384]{2,1,0:T(8,128)(2,1)} %param.13) | copy-start | bytes 589828
  9.5 32.7 %all-to-all-start = ((s32[64,1,2]{2,1,0:T(1,128)}), s32[64,1,2]{2,1,0:T(1,128)S(1)}, u32[]{:S(2)}, u32[]{:S(2)}) async-start(s32[64,1,2]{2,1,0:T(1,128)} %copy.16), calls=%async_computation | async-start | bytes 65536 | tf_op jit(solution)/shard_map/all_to_all | solution.py:44
  42.1 28.0 %all-to-all-start.1 = ((bf16[64,8,384]{2,1,0:T(8,128)(2,1)}), bf16[64,8,384]{2,1,0:T(8,128)(2,1)S(1)}, u32[]{:S(2)}, u32[]{:S(2)}) async-start(bf16[64,8,384]{2,1,0:T(8,128)(2,1)} %copy.19), calls=%async_computation.1 | async-start | bytes 786432 | tf_op jit(solution)/shard_map/all_to_all | solution.py:43
  46.8 52.9 %all-gather.5.cloned.1.call-start = ((), (), s32[]{:S(2)}) async-start(), calls=%async_computation.4 | async-start | bytes 1769472 | tf_op jit(solution)/shard_map/all_gather | solution.py:55
  46.9 52.8 %copy-start.13 = (pred[64]{0:T(512)(128)(4,1)}, pred[64]{0:T(512)(128)(4,1)S(1)}, u32[]{:S(2)}) copy-start(pred[64]{0:T(512)(128)(4,1)S(1)} %broadcast_compare_fusion) | copy-start | bytes 196
  46.9 52.8 %copy-start.9 = (s32[64]{0:T(128)}, s32[64]{0:T(128)S(1)}, u32[]{:S(2)}) copy-start(s32[64]{0:T(128)S(1)} %get-tuple-element.15) | copy-start | bytes 772
  71.1 63.7 %all-gather.11.cloned.1.call-start = ((), (), s32[]{:S(2)}) async-start(), calls=%async_computation.7 | async-start | bytes 1769472 | tf_op jit(solution)/shard_map/all_gather | solution.py:92
  71.5 28.2 %copy-start.11 = (pred[256]{0:T(512)(128)(4,1)}, pred[256]{0:T(512)(128)(4,1)S(1)}, u32[]{:S(2)}) copy-start(pred[256]{0:T(512)(128)(4,1)S(1)} %lt.30) | copy-start | bytes 772
  72.3 198.6 %all-gather.9.cloned.1.call-start = ((), (), s32[]{:S(2)}) async-start(), calls=%async_computation.6 | async-start | bytes 2396160 | tf_op jit(solution)/shard_map/all_gather | solution.py:30
  73.0 351.4 %all-gather.7.cloned.1.call-start = ((), (), s32[]{:S(2)}) async-start(), calls=%async_computation.5 | async-start | bytes 7188480 | tf_op jit(solution)/shard_map/all_gather | solution.py:29
  73.6 452.8 %all-reduce.2.cloned.1.call-start = ((), (), s32[]{:S(2)}) async-start(), calls=%async_computation.8 | async-start | bytes 3145728 | tf_op jit(solution)/shard_map/psum | solution.py:112
  101.4 323.0 %copy-start.1 = (bf16[256,3072]{1,0:T(8,128)(2,1)S(1)}, bf16[256,3072]{1,0:T(8,128)(2,1)}, u32[]{:S(2)}) copy-start(bf16[256,3072]{1,0:T(8,128)(2,1)} %all-gather.5.cloned.1.call-done) | copy-start | bytes 4718596
  101.4 323.0 %copy-start.7 = (f32[3072]{0:T(1024)S(1)}, f32[3072]{0:T(1024)}, u32[]{:S(2)}) copy-start(f32[3072]{0:T(1024)} %param.10) | copy-start | bytes 36868
  101.4 327.8 %copy-start.8 = (f32[256]{0:T(256)}, f32[256]{0:T(256)S(1)}, u32[]{:S(2)}) copy-start(f32[256]{0:T(256)S(1)} %broadcast_multiply_fusion.2) | copy-start | bytes 3076
  424.4 3.7 copy-start.2
  427.3 2.0 copy-start.4
  432.5 8.8 %copy-start.3 = (bf16[32,3,8,8]{2,3,1,0:T(8,128)(2,1)}, bf16[32,3,8,8]{2,3,1,0:T(8,128)(2,1)S(1)}, u32[]{:S(2)}) copy-start(bf16[32,3,8,8]{2,3,1,0:T(8,128)(2,1)S(1)} %divide_convert_fusion) | copy-start | bytes 36868
  446.3 122.6 %reduce-scatter.4.cloned.1.call-start = ((), (), s32[]{:S(2)}) async-start(), calls=%async_computation.9 | async-start | bytes 1769472
  451.3 118.7 %copy-start.6 = (bf16[32,8,384]{2,1,0:T(8,128)(2,1)S(1)}, bf16[32,8,384]{2,1,0:T(8,128)(2,1)}, u32[]{:S(2)}) copy-start(bf16[32,8,384]{2,1,0:T(8,128)(2,1)} %param.13) | copy-start | bytes 589828
  451.3 118.7 %copy-start.12 = (pred[256]{0:T(512)(128)(4,1)S(1)}, pred[256]{0:T(512)(128)(4,1)}, u32[]{:S(2)}) copy-start(pred[256]{0:T(512)(128)(4,1)} %copy-done.11) | copy-start | bytes 772
  451.3 120.7 %copy-start.10 = (s32[64]{0:T(128)S(1)}, s32[64]{0:T(128)}, u32[]{:S(2)}) copy-start(s32[64]{0:T(128)} %copy-done.9) | copy-start | bytes 772
  451.3 120.7 %copy-start.14 = (pred[64]{0:T(512)(128)(4,1)S(1)}, pred[64]{0:T(512)(128)(4,1)}, u32[]{:S(2)}) copy-start(pred[64]{0:T(512)(128)(4,1)} %copy-done.13) | copy-start | bytes 196
  531.3 78.8 %copy-start.15 = (s32[32]{0:T(128)S(1)}, s32[32]{0:T(128)}, u32[]{:S(2)}) copy-start(s32[32]{0:T(128)} %param.9) | copy-start | bytes 388
Sparse Core Ops, SparseCore 0:
  71.2 28.4 all-gather.4
  102.4 32.3 all-gather.10
  137.7 133.0 all-gather.8
  273.8 150.5 all-gather.6
  446.4 79.9 all-reduce.1
  529.1 39.7 reduce-scatter.3
where the time goes:
time: 623 us; the launch traced here: 618 us
  waiting for transfers between devices  492 us (79%)
  blocking collectives  37.4 us (6%)
  matrix products  29.1 us (5%)
  starting transfers between devices  24.3 us (4%)
  between operations  14.4 us (2%)
  other arithmetic  13.3 us (2%)
  local copies, waits for them, and re-layouts  7.03 us (1%)
    all_gather x1, waiting for transfers between devices, per_device(): lax.all_gather(w_qkv, 'dp', axis=1, tiled=True)  150 us
    all_gather x1, waiting for transfers between devices, per_device(): lax.all_gather(w_out, 'dp', axis=1, tiled=True)  136 us
    psum x1, waiting for transfers between devices, per_device(): lax.psum(normed_part.astype(jnp.bfloat16), 'tensor').astype(jnp.float32)  75.1 us
    unnamed x7, waiting for transfers between devices  38.9 us
    all_to_all x1, blocking collectives, per_device(): lax.all_to_all(returning, 'dp', split_axis=0, concat_axis=0, tiled=True)  37.4 us
    all_gather x1, waiting for transfers between devices, per_device(): grad_full = lax.all_gather(grad_rows, 'tensor', axis=1, tiled=True)  31.2 us
    all_gather x1, waiting for transfers between devices, per_device(): gathered = lax.all_gather(local_rows, 'tensor', axis=1, tiled=True)  26 us
    all_to_all x1, waiting for transfers between devices, per_device(): lax.all_to_all(send, 'dp', split_axis=0, concat_axis=0, tiled=True)  23.2 us
  transfers between devices with their start and end apart: 8, of which 8 were waited for; matrix products, arithmetic and copies ran while one was open for 3% of the time, Pallas kernels for 0%

commit v1 on v0

v1 whole, which is shorter than its diff:
```python
import functools

import jax
import jax.numpy as jnp
from jax import lax
from jax.experimental import pallas as pl
from jax.experimental.pallas import tpu as pltpu
from jax.sharding import PartitionSpec as P

HD = 128
D = 3072
NZ, NY, NX = 16, 4, 4
ROWS = 256
W = 384
SHARD = 48
F32 = jnp.float32
BF16 = jnp.bfloat16
NT = (((1,), (1,)), ((), ()))
TN = (((0,), (0,)), ((), ()))
S_COT, S_XG, S_A1, S_M1, S_A2, S_M2 = 0, 7, 14, 29, 44, 47
S_AY, S_AZR, S_AZL = 50, 53, 61
S_BZR, S_BZL, S_BYR, S_BYL, S_BREL = 68, 76, 83, 99, 115
S_RS1, S_RS2, S_SC, S_R1, S_R2 = 131, 133, 139, 146, 149
N_SEM = 164


def dot(a, b, dims=(((1,), (0,)), ((), ()))):
    return lax.dot_general(a, b, dims, preferred_element_type=F32)


def block_kernel(
    meta_ref, x_ref, cot_ref, gain_ref, wqkv_ref, wout_ref, mixed_ref, pg_ref,
    wbuf, xg, cg, send, mid, mid2, recv, msend, mrecv, mall, pick, acc, uacc,
    part_o, part_n, sib_o, sib_n, q_o, q_n, rx_o, rx_n, scal, stats, ret1, got1, ret2, got2,
    ssem, rsem,
):
    dp = lax.axis_index("dp")
    tn = lax.axis_index("tensor")
    z, y = lax.div(dp, NY), lax.rem(dp, NY)
    x, c = lax.div(tn, 2), lax.rem(tn, 2)
    oc = 1 - c

    def at(dz=0, dy=0):
        return lax.rem(z + dz + NZ, NZ) * NY + lax.rem(y + dy + NY, NY)

    def tens(dx, core):
        return lax.rem(x + dx, NX) * 2 + core

    barrier = pltpu.get_barrier_semaphore()
    peers = [(at(k, 0), tn) for k in range(1, NZ)]
    peers += [(at(0, k), tn) for k in range(1, NY)]
    peers += [(dp, tens(k, c)) for k in range(1, NX)]
    peers += [(dp, tens(k, oc)) for k in range(NX)]
    for peer in peers:
        pl.semaphore_signal(barrier, inc=1, device_id=peer, device_id_type=pl.DeviceIdType.MESH)

    pending = []

    def copy(src, dst, sem, to):
        desc = pltpu.make_async_remote_copy(
            src_ref=src, dst_ref=dst, send_sem=ssem.at[sem], recv_sem=rsem.at[sem],
            device_id=to, device_id_type=pl.DeviceIdType.MESH,
        )
        desc.start()
        pending.append(desc)
        return desc

    wbuf[0:3, dp] = wqkv_ref[...]
    wbuf[3, dp] = wout_ref[...]
    cg[tn] = cot_ref[...]
    dest = meta_ref[0:1, :]
    slot = meta_ref[1:2, :]
    pack = (lax.broadcasted_iota(jnp.int32, (512, ROWS), 0) == dest).astype(BF16)
    sorted_rows = dot(pack, x_ref[...]).astype(BF16)
    send[...] = sorted_rows.reshape(NZ, 32, W)
    a_meta = jnp.where(
        lax.broadcasted_iota(jnp.int32, (NZ, ROWS), 0) == lax.shift_right_logical(dest, 5), slot + 1, 0
    ).astype(F32).astype(BF16)
    b_meta = (
        lax.broadcasted_iota(jnp.int32, (128, ROWS), 0) == lax.bitwise_and(dest, 31)
    ).astype(BF16)
    meta_rows = dot(a_meta, b_meta, NT)
    for k in range(NZ):
        msend[k] = meta_rows[k : k + 1, :]

    pl.semaphore_wait(barrier, len(peers))

    a_y = [copy(wbuf.at[3, dp], wbuf.at[3, dp], S_AY + k - 1, (at(0, k), tn)) for k in (1, 2, 3)]

    def b_zr(j):
        r = wbuf.at[pl.ds(0, 3), at(-j)]
        return copy(r, r, S_BZR + j, (at(1), tn))

    def b_zl(j):
        r = wbuf.at[pl.ds(0, 3), at(j)]
        return copy(r, r, S_BZL + j, (at(-1), tn))

    def b_y(d):
        r = wbuf.at[pl.ds(0, 3), at(d)]
        return copy(r, r, S_BYR + d, (at(0, 1), tn)), copy(r, r, S_BYL + d, (at(0, -1), tn))

    def b_relay(d, up):
        r = wbuf.at[pl.ds(0, 3), at(d, -1 if up else 1)]
        return copy(r, r, S_BREL + d, (at(0, 1 if up else -1), tn))

    def a_zr(j):
        r = wbuf.at[3, pl.ds(lax.rem(z - j + NZ, NZ) * NY, NY)]
        return copy(r, r, S_AZR + j, (at(1), tn))

    def a_zl(j):
        r = wbuf.at[3, pl.ds(lax.rem(z + j, NZ) * NY, NY)]
        return copy(r, r, S_AZL + j, (at(-1), tn))

    zr, zl, yy, rel, azr, azl = {}, {}, {}, {}, {}, {}
    zr[0], zl[0] = b_zr(0), b_zl(0)
    yy[0] = b_y(0)

    a1, m1 = [], []
    for k in range(1, NZ):
        p = lax.rem(z + k, NZ)
        m1.append(copy(msend.at[p], mrecv.at[z], S_M1 + k - 1, (at(k), tn)))
        a1.append(copy(send.at[p], mid.at[z], S_A1 + k - 1, (at(k), tn)))
    mid[z] = send[z]
    mrecv[z] = msend[z]

    def gather_start(buf, base):
        own = buf.at[tn]
        sib = copy(own, own, base, (dp, tens(0, oc)))
        return [sib] + [copy(own, own, base + k, (dp, tens(k, c))) for k in (1, 2, 3)]

    def gather_pass(buf, base, ds):
        out = []
        for k in (1, 2, 3):
            ds[k].wait_recv()
            r = buf.at[tens(NX - k, c)]
            out.append(copy(r, r, base + 3 + k, (dp, tens(0, oc))))
        return out

    cot_d = gather_start(cg, S_COT)
    a2, m2, xg_d, xg_f, cot_f = [], [], [], [], []

    def tiles_second():
        for d in a1 + m1:
            d.wait_recv()
        tiles = mid[...].astype(F32)
        for q in range(NY):
            mid2[q] = jnp.concatenate(
                [tiles[s, q * 8 : q * 8 + 8, :] for s in range(NZ)], axis=0
            ).astype(BF16)
        for k in (1, 2, 3):
            p = lax.rem(y + k, NY)
            m2.append(copy(mrecv, mall.at[y], S_M2 + k - 1, (at(0, k), tn)))
            a2.append(copy(mid2.at[p], recv.at[y], S_A2 + k - 1, (at(0, k), tn)))
        recv[y] = mid2[y]
        mall[y] = mrecv[...]

    def tiles_last():
        for d in a2 + m2:
            d.wait_recv()
        lane = lax.broadcasted_iota(jnp.int32, (128, 128), 1)
        sel = (
            lax.broadcasted_iota(jnp.int32, (128, 128), 0) == y * 8 + lax.bitwise_and(lane, 7)
        ).astype(BF16)
        mine = (
            lax.broadcasted_iota(jnp.int32, (NZ, 128), 0)
            == lax.shift_right_logical(lax.broadcasted_iota(jnp.int32, (NZ, 128), 1), 3)
        )
        parts = []
        for q in range(NY):
            rows = jnp.concatenate([mall[q, s] for s in range(NZ)], axis=0)
            t = dot(rows.astype(BF16), sel)
            parts.append(jnp.sum(jnp.where(mine, t, 0.0), axis=0, keepdims=True))
        where_to = jnp.concatenate(parts, axis=1).astype(jnp.int32) - 1
        picked = (lax.broadcasted_iota(jnp.int32, (ROWS, 512), 0) == where_to).astype(BF16)
        pick[...] = picked
        xg[tn] = dot(picked, recv[...].reshape(512, W)).astype(BF16)
        xg_d.extend(gather_start(xg, S_XG))

    for j in range(1, 9):
        zr[j - 1].wait_recv()
        if j < 8:
            zr[j] = b_zr(j)
        yy[NZ - j] = b_y(NZ - j)
        if j < 8:
            zl[j - 1].wait_recv()
            if j < 7:
                zl[j] = b_zl(j)
            yy[j] = b_y(j)
        if j == 1:
            for d in a_y:
                d.wait_recv()
            azr[0], azl[0] = a_zr(0), a_zl(0)
        else:
            azr[j - 2].wait_recv()
            azr[j - 1] = a_zr(j - 1)
            azl[j - 2].wait_recv()
            if j < 8:
                azl[j - 1] = a_zl(j - 1)
        if j == 1:
            yy[0][1].wait_recv()
            rel[0] = b_relay(0, False)
        else:
            d = NZ - (j - 1)
            yy[d][0].wait_recv()
            rel[d] = b_relay(d, True)
            d = j - 1
            yy[d][1].wait_recv()
            rel[d] = b_relay(d, False)
        if j == 3:
            cot_f = gather_pass(cg, S_COT, cot_d)
        if j == 4:
            tiles_second()
        if j == 5:
            tiles_last()
        if j == 7:
            xg_f = gather_pass(xg, S_XG, xg_d)
    yy[8][0].wait_recv()
    rel[8] = b_relay(8, True)

    xg_d[0].wait_recv()
    for d in xg_f:
        d.wait_recv()
    cot_d[0].wait_recv()
    for d in cot_f:
        d.wait_recv()
    total = jnp.zeros((ROWS, 1), F32)
    for t in range(8):
        total = total + jnp.sum(xg[t].astype(F32), axis=1, keepdims=True)
    mean = total * (1.0 / D)
    sq = jnp.zeros((ROWS, 1), F32)
    for t in range(8):
        cen = xg[t].astype(F32) - mean
        sq = sq + jnp.sum(cen * cen, axis=1, keepdims=True)
    inv_std = lax.rsqrt(sq * (1.0 / D) + 1e-06)
    live_col = jnp.sum(pick[...].astype(F32), axis=1, keepdims=True)
    eye = lax.broadcasted_iota(jnp.int32, (ROWS, ROWS), 0) == lax.broadcasted_iota(
        jnp.int32, (ROWS, ROWS), 1
    )
    live_row = jnp.sum(jnp.where(eye, live_col, 0.0), axis=0, keepdims=True)
    stats[0] = jnp.broadcast_to(mean, (ROWS, 128))
    stats[1] = jnp.broadcast_to(inv_std, (ROWS, 128))
    stats[2] = jnp.broadcast_to(live_col, (ROWS, 128))

    azr[7].wait_recv()
    for j in range(9):
        d = (NZ - j) % NZ
        if j > 0:
            yy[d][1].wait_recv()
            rel[d].wait_recv()
        if j < 8:
            yy[j][0].wait_recv()
            rel[j].wait_recv()

    acc[...] = jnp.zeros_like(acc)
    uacc[...] = jnp.zeros_like(uacc)

    def project(t, carry):
        m = stats[0][:, 0:1]
        inv = stats[1][:, 0:1]
        live = stats[2][:, 0:1]
        gain = gain_ref[t]
        normed = ((xg[t].astype(F32) - m) * inv * gain).astype(BF16)
        g0 = gain.astype(BF16)
        rest = gain - g0.astype(F32)
        g1 = rest.astype(BF16)
        g2 = (rest - g1.astype(F32)).astype(BF16)
        gains = jnp.concatenate(
            [g0.astype(F32), g1.astype(F32), g2.astype(F32), jnp.zeros((13, W), F32)], axis=0
        ).astype(BF16)
        for i in range(3):
            wt = wbuf[i, pl.ds(t * 8, 8)].reshape(W, W)
            acc[i] += dot(normed, wt)
            uacc[i] += dot(gains, wt)
        grad = jnp.where(live > 0.5, cg[t], jnp.zeros((), BF16))
        acc[3] += dot(grad, wbuf[3, pl.ds(t * 8, 8)].reshape(W, W))
        return carry

    lax.fori_loop(0, 8, project, 0)

    row_img = lax.shift_right_logical(lax.broadcasted_iota(jnp.int32, (ROWS, ROWS), 0), 3)
    col_img = lax.shift_right_logical(lax.broadcasted_iota(jnp.int32, (ROWS, ROWS), 1), 3)
    ok = (row_img == col_img) & (live_row > 0.5)
    scale = HD ** (-0.5)
    s1 = jnp.zeros((ROWS, 1), F32)
    s2 = jnp.zeros((ROWS, 1), F32)
    attn, grads = [], [[], [], []]
    for h in range(3):
        cols = slice(h * HD, (h + 1) * HD)
        qf, kf, vf = (acc[i][:, cols] for i in range(3))
        q, k, v = qf.astype(BF16), kf.astype(BF16), vf.astype(BF16)
        ag = acc[3][:, cols].astype(BF16)
        sc = jnp.where(ok, dot(q, k, NT) * scale, -1e30)
        ex = jnp.exp(sc - jnp.max(sc, axis=1, keepdims=True))
        probs = (ex / jnp.sum(ex, axis=1, keepdims=True)).astype(BF16)
        attn.append(dot(probs, v).astype(BF16))
        dprobs = dot(ag, v, NT)
        probs32 = probs.astype(F32)
        inner = jnp.sum(dprobs * probs32, axis=1, keepdims=True)
        sg = (probs32 * (dprobs - inner) * scale).astype(BF16)
        vg = dot(probs, ag, TN).astype(BF16)
        qg = dot(sg, k).astype(BF16)
        kg = dot(sg, q, TN).astype(BF16)
        for i, (g, f) in enumerate(((qg, qf), (kg, kf), (vg, vf))):
            grads[i].append(g)
            g32 = g.astype(F32)
            u = jnp.sum(uacc[i][:, cols], axis=0, keepdims=True)
            s1 = s1 + jnp.sum(g32 * u, axis=1, keepdims=True)
            s2 = s2 + jnp.sum(g32 * f, axis=1, keepdims=True)
    attn = jnp.concatenate(attn, axis=1)
    grads = [jnp.concatenate(g, axis=1) for g in grads]
    s1r = jnp.sum(jnp.where(eye, s1, 0.0), axis=0, keepdims=True)
    s2r = jnp.sum(jnp.where(eye, s2, 0.0), axis=0, keepdims=True)
    scal[tn] = jnp.concatenate([s1r, s2r, jnp.zeros((6, ROWS), F32)], axis=0)
    own_s = scal.at[tn]
    sc_d = [copy(own_s, own_s, S_SC + k - 1, (dp, tens(k, c))) for k in (1, 2, 3)]
    sc_d += [copy(own_s, own_s, S_SC + 3 + k, (dp, tens(k, oc))) for k in range(4)]

    for t in range(8):
        wts = [wbuf[i, t * 8 : t * 8 + 8].reshape(W, W) for i in range(3)]
        p = dot(grads[0], wts[0], NT) + dot(grads[1], wts[1], NT) + dot(grads[2], wts[2], NT)
        part_n[t % 2, t // 2] = p.astype(BF16)
    sib_nd = copy(part_n.at[oc], sib_n, S_RS1, (dp, tens(0, oc)))
    for t in range(8):
        part_o[t % 2, t // 2] = dot(
            attn, wbuf[3, t * 8 : t * 8 + 8].reshape(W, W), NT
        ).astype(BF16)
    sib_od = copy(part_o.at[oc], sib_o, S_RS1 + 1, (dp, tens(0, oc)))

    def fold(part, sib, q, rx, base):
        ds = []
        for k in (2, 1, 3):
            xx = lax.rem(x + k, NX)
            q[xx] = (part[c, xx].astype(F32) + sib[xx].astype(F32)).astype(BF16)
            ds.append(copy(q.at[xx], rx.at[k - 1], base + k - 1, (dp, tens(k, c))))
        return ds

    sib_nd.wait_recv()
    rs_n = fold(part_n, sib_n, q_n, rx_n, S_RS2)
    sib_od.wait_recv()
    rs_o = fold(part_o, sib_o, q_o, rx_o, S_RS2 + 3)

    def summed(part, sib, rx):
        s = part[c, x].astype(F32) + sib[x].astype(F32)
        return s + rx[0].astype(F32) + rx[1].astype(F32) + rx[2].astype(F32)

    for d in sc_d:
        d.wait_recv()
    sums = scal[0]
    for t in range(1, 8):
        sums = sums + scal[t]
    mean1 = jnp.sum(jnp.where(eye, sums[0:1, :], 0.0), axis=1, keepdims=True) * (1.0 / D)
    mean2 = jnp.sum(jnp.where(eye, sums[1:2, :], 0.0), axis=1, keepdims=True) * (1.0 / D)
    live = live_col > 0.5
    local = xg[tn].astype(F32)
    unit = (local - mean) * inv_std
    for d in rs_n:
        d.wait_recv()
    ng = summed(part_n, sib_n, rx_n)
    back = inv_std * (ng * gain_ref[tn] - mean1 - unit * mean2)
    moved = jnp.where(live, cot_ref[...].astype(F32) + back, 0.0).astype(BF16)

    ret1[...] = dot(pick[...], moved, TN).astype(BF16).reshape(NY, 128, W)
    r1 = []
    for k in (1, 2, 3):
        p = lax.rem(y + k, NY)
        r1.append(copy(ret1.at[p], got1.at[y], S_R1 + k - 1, (at(0, k), tn)))
    got1[y] = ret1[y]
    for d in r1:
        d.wait_recv()
    tiles = got1[...].astype(F32)
    for s in range(NZ):
        ret2[s] = jnp.concatenate(
            [tiles[q, s * 8 : s * 8 + 8, :] for q in range(NY)], axis=0
        ).astype(BF16)
    r2 = []
    for k in range(1, NZ):
        p = lax.rem(z + k, NZ)
        r2.append(copy(ret2.at[p], got2.at[z], S_R2 + k - 1, (at(k), tn)))
    got2[z] = ret2[z]

    for d in rs_o:
        d.wait_recv()
    branch = summed(part_o, sib_o, rx_o)
    mixed_ref[...] = jnp.where(live, local + branch, 0.0).astype(BF16)

    for d in r2:
        d.wait_recv()
    pack2 = (lax.broadcasted_iota(jnp.int32, (512, ROWS), 0) == meta_ref[0:1, :]).astype(BF16)
    pg_ref[...] = dot(pack2, got2[...].reshape(512, W), TN).astype(BF16)
    for d in pending:
        d.wait_send()


def per_device(patches, counts, target, ln_gain, w_qkv, w_out, cotangent):
    images, slot_len, width = patches.shape
    pos = jnp.arange(slot_len, dtype=jnp.int32)[None, :]
    dest = (target[:, None] * slot_len + pos).reshape(1, ROWS)
    ids = jnp.arange(images, dtype=jnp.int32)[:, None] * slot_len + pos
    slot = jnp.where(pos < counts[:, None], ids, -1).reshape(1, ROWS)
    meta = jnp.concatenate([dest, slot, jnp.zeros((6, ROWS), jnp.int32)], axis=0)
    vm = pl.BlockSpec(memory_space=pltpu.VMEM)
    b = lambda *s: pltpu.VMEM(s, BF16)
    f = lambda *s: pltpu.VMEM(s, F32)
    scratch = [
        b(4, 64, SHARD, W), b(8, ROWS, W), b(8, ROWS, W),
        b(NZ, 32, W), b(NZ, 32, W), b(NY, 128, W), b(NY, 128, W),
        f(NZ, 1, 128), f(NZ, 1, 128), f(NY, NZ, 1, 128),
        b(ROWS, 512), f(4, ROWS, W), f(3, 16, W),
        b(2, 4, ROWS, W), b(2, 4, ROWS, W), b(4, ROWS, W), b(4, ROWS, W),
        b(4, ROWS, W), b(4, ROWS, W), b(3, ROWS, W), b(3, ROWS, W),
        f(8, 8, ROWS), f(3, ROWS, 128),
        b(NY, 128, W), b(NY, 128, W), b(NZ, 32, W), b(NZ, 32, W),
        pltpu.SemaphoreType.DMA((N_SEM,)), pltpu.SemaphoreType.DMA((N_SEM,)),
    ]
    mixed, grad = pl.pallas_call(
        block_kernel,
        out_shape=[jax.ShapeDtypeStruct((ROWS, W), BF16)] * 2,
        in_specs=[vm] * 6,
        out_specs=[vm] * 2,
        scratch_shapes=scratch,
        compiler_params=pltpu.CompilerParams(
            collective_id=0, has_side_effects=True, vmem_limit_bytes=56 << 20
        ),
        name="attention_block",
    )(
        meta, patches.reshape(ROWS, width), cotangent.reshape(ROWS, width),
        ln_gain.reshape(8, 1, W), w_qkv, w_out.T,
    )
    return mixed.reshape(patches.shape), grad.reshape(patches.shape)


def solution(mesh):
    in_specs = (
        P("dp", None, "tensor"), P("dp"), P("dp"), P(), P(None, "dp", "tensor"),
        P("tensor", "dp"), P("dp", None, "tensor"),
    )
    out_specs = (P("dp", None, "tensor"), P("dp", None, "tensor"))
    return jax.shard_map(
        per_device, mesh=mesh, in_specs=in_specs, out_specs=out_specs, check_vma=False
    )
```

time: 623 us -> 162 us (0.26)
  waiting for transfers between devices: 492 us -> 0 us
  Pallas kernels: 0 us -> 156 us
  blocking collectives: 37.4 us -> 0 us
  matrix products: 29.1 us -> 0 us
  starting transfers between devices: 24.3 us -> 0 us
  between operations: 14.4 us -> 0.66 us
  other arithmetic: 13.3 us -> 0.82 us
    all_gather x4 -> x0, waiting for transfers between devices: 344 us -> none  [the longest x1 150 us: per_device(): lax.all_gather(w_qkv, 'dp', axis=1, tiled=True)]
    pallas_call x0 -> x1, Pallas kernels: none -> 156 us  [per_device(): pl.pallas_call(block_kernel, out_shape=[jax.ShapeDtypeStruct((ROWS, W), B...]
    psum x1 -> x0, waiting for transfers between devices: 75.1 us -> none  [per_device(): lax.psum(normed_part.astype(jnp.bfloat16), 'tensor').astype(jnp.float32)]
    unnamed x7 -> x0, waiting for transfers between devices: 38.9 us -> none
    all_to_all x1 -> x0, blocking collectives: 37.4 us -> none  [per_device(): lax.all_to_all(returning, 'dp', split_axis=0, concat_axis=0, tiled=True)]
    all_to_all x2 -> x0, waiting for transfers between devices: 34.5 us -> none  [the longest x1 23.2 us: per_device(): lax.all_to_all(send, 'dp', split_axis=0, concat_axis=0, tiled=True)]
    dot_general x15 -> x0, matrix products: 27.7 us -> none  [the longest x4 15.2 us: right_dot(): lax.dot_general(left, weight, (((1,), (1,)), ((), ())), preferred_element...]
    all_to_all x2 -> x0, starting transfers between devices: 23.9 us -> none  [the longest x1 19.3 us: per_device(): lax.all_to_all(meta, 'dp', split_axis=0, concat_axis=0, tiled=True)]
  transfers between devices with their start and end apart: 8 -> 0, of which waited for: 8 -> 0; matrix products, arithmetic and copies ran while one was open for 3% -> 0% of each run, Pallas kernels for 0% -> 0%
where the time goes in v1:
time: 162 us
  Pallas kernels  156 us (96%)
  local copies, waits for them, and re-layouts  3.9 us (2%)
    pallas_call x1, Pallas kernels, per_device(): pl.pallas_call(block_kernel, out_shape=[jax.ShapeDtypeStruct((ROWS, W), B...  156 us
    unnamed x8, local copies, waits for them, and re-layouts  3.64 us

profile of v1, /device:TPU:1, one launch (start us, length us, event | category | flops | bytes accessed | tf_op | source)
XLA Modules:
  0.0 161.5 jit_solution(16835486482167426431)
XLA Ops:
  0.6 0.0 copy-start.2
  0.6 0.6 copy-done.2
  1.3 0.1 pad.2.clone
  1.4 0.0 copy-start.1
  1.4 0.6 copy-done.1
  2.0 0.1 add_select_fusion
  2.1 0.1 select_n.15
  2.2 0.1 iota_add_fusion
  2.3 0.1 add.49
  2.4 0.7 add_add_fusion.meta_ref
  3.0 156.1 %attention_block.1 = (bf16[256,384]{1,0:T(8,128)(2,1)}, bf16[256,384]{1,0:T(8,128)(2,1)}) custom-call(s32[8,256]{1,0:T(8,128)} %add_add_fusion.meta_ref, bf16[256,384]{1,0:T(8,128)(2,1)} %bitcast.6, bf16[256,384]{1,0:T(8,128)(2,1)} %bitcast.7, f32[8,1,384]{2,1,0:T(1,128)} %bitcast.11, bf16[3,48,384]{2,1,0:T(8,128)(2,1)} %wqkv_ref.1, bf16[48,384]{1,0:T(8,128)(2,1)} %bitcast.10), custom_call_target="tpu_custom_call" | custom-call | tf_op jit(solution)/shard_map/attention_block/pallas_call | solution.py:415
  159.2 0.0 copy-start
  159.2 1.7 %copy.11 = bf16[32,8,384]{2,1,0:T(8,128)(2,1)} copy(bf16[32,8,384]{2,1,0:T(8,128)(2,1)} %bitcast.9) | data formatting | bytes 393216
  160.8 0.0 copy-done
  160.8 0.7 copy.12
  (3 shorter events, 0.0 us)
Async XLA Ops:
  0.6 0.7 copy-start.2
  1.4 0.7 copy-start.1
  159.2 1.7 %copy-start = (bf16[256,384]{1,0:T(8,128)(2,1)S(1)}, bf16[256,384]{1,0:T(8,128)(2,1)}, u32[]{:S(2)}) copy-start(bf16[256,384]{1,0:T(8,128)(2,1)} %get-tuple-element.5) | copy-start | bytes 589828

commit v2 on v1

v2 whole, which is shorter than its diff:
```python
import jax
import jax.numpy as jnp
from jax import lax
from jax.experimental import pallas as pl
from jax.experimental.pallas import tpu as pltpu
from jax.sharding import PartitionSpec as P

HD = 128
D = 3072
NZ, NY, NX = 16, 4, 4
ROWS = 256
W = 384
SHARD = 48
SLAB = 192
F32 = jnp.float32
BF16 = jnp.bfloat16
NT = (((1,), (1,)), ((), ()))
TN = (((0,), (0,)), ((), ()))
S_COT = 0
S_XG = 7
S_A1 = 14
S_M1 = 29
S_A2 = 44
S_M2 = 47
S_AY = 50
S_AZR = 53
S_AZL = 61
S_BZR = 68
S_BZL = 76
S_BYR = 83
S_BYL = 99
S_BREL = 115
S_NS = 131
S_NX = 135
S_OS = 144
S_OX = 145
S_SC = 148
S_R1 = 155
S_R2 = 164
N_SEM = 209


def dot(a, b, dims=(((1,), (0,)), ((), ()))):
    return lax.dot_general(a, b, dims, preferred_element_type=F32)


def block_kernel(
    meta_ref, x_ref, cot_ref, gain_ref, wqkv_ref, wout_ref, mixed_ref, pg_ref,
    wbuf, xg, cg, nb, gb, send, mid, mid2, recv, msend, mrecv, mall, pick, pick_t, pack_t,
    acc, part_n, part_o, sib_n, sib_o, q_n, q_o, rx_n, rx_o, scal,
    ret1, got1, ret2, got2,
    ssem, rsem,
):
    dp = lax.axis_index("dp")
    tn = lax.axis_index("tensor")
    z, y = lax.div(dp, NY), lax.rem(dp, NY)
    x, c = lax.div(tn, 2), lax.rem(tn, 2)
    oc = 1 - c

    def at(dz=0, dy=0):
        return lax.rem(z + dz + NZ, NZ) * NY + lax.rem(y + dy + NY, NY)

    def tens(dx, core):
        return lax.rem(x + dx, NX) * 2 + core

    barrier = pltpu.get_barrier_semaphore()
    peers = [(at(k, 0), tn) for k in range(1, NZ)]
    peers += [(at(0, k), tn) for k in range(1, NY)]
    peers += [(dp, tens(k, c)) for k in range(1, NX)]
    peers += [(dp, tens(k, oc)) for k in range(NX)]
    for peer in peers:
        pl.semaphore_signal(barrier, inc=1, device_id=peer, device_id_type=pl.DeviceIdType.MESH)

    pending = []

    def copy(src, dst, sem, to):
        desc = pltpu.make_async_remote_copy(
            src_ref=src, dst_ref=dst, send_sem=ssem.at[sem], recv_sem=rsem.at[sem],
            device_id=to, device_id_type=pl.DeviceIdType.MESH,
        )
        desc.start()
        pending.append(desc)
        return desc

    def rows_of(p):
        return pl.ds(pl.multiple_of(p * SHARD, SHARD), SHARD)

    def slab(zz):
        return pl.ds(pl.multiple_of(zz * SLAB, SLAB), SLAB)

    wbuf[0:3, rows_of(dp)] = wqkv_ref[...]
    wbuf[3, rows_of(dp)] = wout_ref[...]
    cg[tn] = cot_ref[...]
    eye = lax.broadcasted_iota(jnp.int32, (ROWS, ROWS), 0) == lax.broadcasted_iota(
        jnp.int32, (ROWS, ROWS), 1
    )
    pl.semaphore_wait(barrier, len(peers))

    def b_zr(j):
        r = wbuf.at[pl.ds(0, 3), rows_of(at(-j))]
        return copy(r, r, S_BZR + j, (at(1), tn))

    def b_zl(j):
        r = wbuf.at[pl.ds(0, 3), rows_of(at(j))]
        return copy(r, r, S_BZL + j, (at(-1), tn))

    def b_y(d):
        r = wbuf.at[pl.ds(0, 3), rows_of(at(d))]
        return copy(r, r, S_BYR + d, (at(0, 1), tn)), copy(r, r, S_BYL + d, (at(0, -1), tn))

    def b_relay(d, up):
        r = wbuf.at[pl.ds(0, 3), rows_of(at(d, -1 if up else 1))]
        return copy(r, r, S_BREL + d, (at(0, 1 if up else -1), tn))

    def a_zr(j):
        r = wbuf.at[3, slab(lax.rem(z - j + NZ, NZ))]
        return copy(r, r, S_AZR + j, (at(1), tn))

    def a_zl(j):
        r = wbuf.at[3, slab(lax.rem(z + j, NZ))]
        return copy(r, r, S_AZL + j, (at(-1), tn))

    zr, zl, yy, rel, azr, azl = {}, {}, {}, {}, {}, {}
    a_y, a1, m1, a2, m2, cot_d, cot_f, xg_d, xg_f = [], [], [], [], [], [], [], [], []

    def tiles_sort():
        dest = meta_ref[0:1, :]
        slot = meta_ref[1:2, :]
        pack = (lax.broadcasted_iota(jnp.int32, (512, ROWS), 0) == dest).astype(BF16)
        send[...] = dot(pack, x_ref[...]).astype(BF16).reshape(NZ, 32, W)
        pack_t[...] = dot(eye.astype(BF16), pack, NT).astype(BF16)
        a_meta = jnp.where(
            lax.broadcasted_iota(jnp.int32, (NZ, ROWS), 0) == lax.shift_right_logical(dest, 5),
            slot + 1, 0,
        ).astype(F32).astype(BF16)
        b_meta = (
            lax.broadcasted_iota(jnp.int32, (128, ROWS), 0) == lax.bitwise_and(dest, 31)
        ).astype(BF16)
        meta_rows = dot(a_meta, b_meta, NT)
        for k in range(NZ):
            msend[k] = meta_rows[k : k + 1, :]
        mid[z] = send[z]
        mrecv[z] = msend[z]

    def tiles_first(*ks):
        for k in ks:
            p = lax.rem(z + k, NZ)
            m1.append(copy(msend.at[p], mrecv.at[z], S_M1 + k - 1, (at(k), tn)))
            a1.append(copy(send.at[p], mid.at[z], S_A1 + k - 1, (at(k), tn)))

    def tiles_second():
        for d in a1 + m1:
            d.wait_recv()
        tiles = mid[...].astype(F32)
        for q in range(NY):
            mid2[q] = jnp.concatenate(
                [tiles[s, q * 8 : q * 8 + 8, :] for s in range(NZ)], axis=0
            ).astype(BF16)
        for k in (1, 2, 3):
            p = lax.rem(y + k, NY)
            m2.append(copy(mrecv, mall.at[y], S_M2 + k - 1, (at(0, k), tn)))
            a2.append(copy(mid2.at[p], recv.at[y], S_A2 + k - 1, (at(0, k), tn)))
        recv[y] = mid2[y]
        mall[y] = mrecv[...]

    def tiles_last():
        for d in a2 + m2:
            d.wait_recv()
        lane = lax.broadcasted_iota(jnp.int32, (128, 128), 1)
        sel = (
            lax.broadcasted_iota(jnp.int32, (128, 128), 0) == y * 8 + lax.bitwise_and(lane, 7)
        ).astype(BF16)
        mine = (
            lax.broadcasted_iota(jnp.int32, (NZ, 128), 0)
            == lax.shift_right_logical(lax.broadcasted_iota(jnp.int32, (NZ, 128), 1), 3)
        )
        parts = []
        for q in range(NY):
            rows = jnp.concatenate([mall[q, s] for s in range(NZ)], axis=0)
            t = dot(rows.astype(BF16), sel)
            parts.append(jnp.sum(jnp.where(mine, t, 0.0), axis=0, keepdims=True))
        where_to = jnp.concatenate(parts, axis=1).astype(jnp.int32) - 1
        picked = (lax.broadcasted_iota(jnp.int32, (ROWS, 512), 0) == where_to).astype(BF16)
        pick[...] = picked
        xg[tn] = dot(picked, recv[...].reshape(512, W)).astype(BF16)
        xg_d.extend(gather_start(xg, S_XG))
        eye512 = lax.broadcasted_iota(jnp.int32, (512, 512), 0) == lax.broadcasted_iota(
            jnp.int32, (512, 512), 1
        )
        pick_t[...] = dot(eye512.astype(BF16), picked, NT).astype(BF16)
        live_col = jnp.sum(picked.astype(F32), axis=1, keepdims=True)
        st["live_row"] = jnp.sum(jnp.where(eye, live_col, 0.0), axis=0, keepdims=True)
        st["live"] = live_col > 0.5

    def gather_start(buf, base):
        own = buf.at[tn]
        sib = copy(own, own, base, (dp, tens(0, oc)))
        return [sib] + [copy(own, own, base + k, (dp, tens(k, c))) for k in (1, 2, 3)]

    def gather_pass(buf, base, ds):
        out = []
        for k in (1, 2, 3):
            ds[k].wait_recv()
            r = buf.at[tens(NX - k, c)]
            out.append(copy(r, r, base + 3 + k, (dp, tens(0, oc))))
        return out

    def a_first():
        for k in (1, 2, 3):
            r = wbuf.at[3, rows_of(dp)]
            a_y.append(copy(r, r, S_AY + k - 1, (at(0, k), tn)))

    def b_step(j):
        if j == 0:
            zr[0], zl[0] = b_zr(0), b_zl(0)
            yy[0] = b_y(0)
            return
        zr[j - 1].wait_recv()
        if j < 8:
            zr[j] = b_zr(j)
        yy[NZ - j] = b_y(NZ - j)
        if j < 8:
            zl[j - 1].wait_recv()
            if j < 7:
                zl[j] = b_zl(j)
            yy[j] = b_y(j)

    def relay_step(j):
        if j > 0:
            d = NZ - j
            yy[d][0].wait_recv()
            rel[d] = b_relay(d, True)
        if j < 8:
            yy[j][1].wait_recv()
            rel[j] = b_relay(j, False)

    def a_step(j):
        if j == 0:
            for d in a_y:
                d.wait_recv()
        else:
            azr[j - 1].wait_recv()
            if j < 8:
                azl[j - 1].wait_recv()
        if j < 8:
            azr[j] = a_zr(j)
        if j < 7:
            azl[j] = a_zl(j)

    def b_done(j):
        d = (NZ - j) % NZ
        if j > 0:
            yy[d][1].wait_recv()
            rel[d].wait_recv()
        if j < 8:
            yy[j][0].wait_recv()
            rel[j].wait_recv()

    def project_qkv(j):
        b_done(j)
        for zz in {0: (z,), 8: (lax.rem(z + 8, NZ),)}.get(
            j, (lax.rem(z + j, NZ), lax.rem(z - j + NZ, NZ))
        ):
            rows = nb[zz]
            for i in range(3):
                p = dot(rows, wbuf[i, slab(zz)])
                acc[i] = p if j == 0 else acc[i] + p

    def project_grad(j):
        for zz in {0: (z,), 8: (lax.rem(z + 8, NZ),)}.get(
            j, (lax.rem(z + j, NZ), lax.rem(z - j + NZ, NZ))
        ):
            p = dot(gb[zz], wbuf[3, slab(zz)])
            acc[3, 0:ROWS] = p if j == 0 else acc[3, 0:ROWS] + p

    def grads_ready():
        cot_d[0].wait_recv()
        for d in cot_f:
            d.wait_recv()
        for t in range(8):
            g = jnp.where(st["live"], cg[t], jnp.zeros((), BF16))
            gb[2 * t] = g[:, :SLAB]
            gb[2 * t + 1] = g[:, SLAB:]

    def norm():
        xg_d[0].wait_recv()
        for d in xg_f:
            d.wait_recv()
        total = jnp.zeros((ROWS, 1), F32)
        for t in range(8):
            total = total + jnp.sum(xg[t].astype(F32), axis=1, keepdims=True)
        mean = total * (1.0 / D)
        sq = jnp.zeros((ROWS, 1), F32)
        for t in range(8):
            cen = xg[t].astype(F32) - mean
            sq = sq + jnp.sum(cen * cen, axis=1, keepdims=True)
        inv_std = lax.rsqrt(sq * (1.0 / D) + 1e-06)
        for t in range(8):
            gain = gain_ref[t]
            normed = ((xg[t].astype(F32) - mean) * inv_std * gain).astype(BF16)
            g0 = gain.astype(BF16).astype(F32)
            g1 = (gain - g0).astype(BF16).astype(F32)
            g2 = (gain - g0 - g1).astype(BF16).astype(F32)
            gains = jnp.concatenate([g0, g1, g2, jnp.zeros((13, W), F32)], axis=0).astype(BF16)
            for half in range(2):
                lanes = slice(half * SLAB, (half + 1) * SLAB)
                nb[2 * t + half, 0:ROWS] = normed[:, lanes]
                nb[2 * t + half, ROWS:] = gains[:, lanes]
        st["mean"], st["inv_std"] = mean, inv_std

    st = {}

    def cot_start():
        cot_d.extend(gather_start(cg, S_COT))

    def cot_pass():
        cot_f.extend(gather_pass(cg, S_COT, cot_d))

    def x_pass():
        xg_f.extend(gather_pass(xg, S_XG, xg_d))

    b_step(0)
    a_first()
    cot_start()
    tiles_sort()
    tiles_first(8,7,9,6,10)
    b_step(1)
    tiles_first(5,11,4,12,3)
    relay_step(0)
    b_step(2)
    tiles_first(13,2,14,1,15)
    relay_step(1)
    a_step(0)
    b_step(3)
    relay_step(2)
    a_step(1)
    b_step(4)
    cot_pass()
    tiles_second()
    relay_step(3)
    a_step(2)
    b_step(5)
    relay_step(4)
    a_step(3)
    b_step(6)
    tiles_last()
    relay_step(5)
    a_step(4)
    b_step(7)
    grads_ready()
    relay_step(6)
    a_step(5)
    x_pass()
    b_step(8)
    norm()
    relay_step(7)
    a_step(6)
    project_qkv(0)
    project_qkv(1)
    relay_step(8)
    project_qkv(2)
    a_step(7)
    project_qkv(3)
    project_qkv(4)
    a_step(8)
    project_qkv(5)
    project_qkv(6)
    for j in range(9):
        project_grad(j)
    project_qkv(7)
    project_qkv(8)
    live, live_row, mean, inv_std = st["live"], st["live_row"], st["mean"], st["inv_std"]

    half_rows = ROWS // 2
    row_img = lax.shift_right_logical(
        lax.broadcasted_iota(jnp.int32, (half_rows, half_rows), 0), 3
    )
    col_img = lax.shift_right_logical(
        lax.broadcasted_iota(jnp.int32, (half_rows, half_rows), 1), 3
    )
    same = row_img == col_img
    scale = HD ** (-0.5)
    attn_rows, grad_rows, s1_rows, s2_rows = [], [], [], []
    for r in range(2):
        rs = slice(r * half_rows, (r + 1) * half_rows)
        ok = same & (live_row[:, rs] > 0.5)
        s1 = jnp.zeros((half_rows, 1), F32)
        s2 = jnp.zeros((half_rows, 1), F32)
        attn, grads = [], [[], [], []]
        for h in range(3):
            cols = slice(h * HD, (h + 1) * HD)
            qf, kf, vf = (acc[i, rs, cols] for i in range(3))
            q, k, v = qf.astype(BF16), kf.astype(BF16), vf.astype(BF16)
            ag = acc[3, rs, cols].astype(BF16)
            sc = jnp.where(ok, dot(q, k, NT) * scale, -1e30)
            ex = jnp.exp(sc - jnp.max(sc, axis=1, keepdims=True))
            probs = (ex / jnp.sum(ex, axis=1, keepdims=True)).astype(BF16)
            attn.append(dot(probs, v).astype(BF16))
            dprobs = dot(ag, v, NT)
            probs32 = probs.astype(F32)
            inner = jnp.sum(dprobs * probs32, axis=1, keepdims=True)
            sg = (probs32 * (dprobs - inner) * scale).astype(BF16)
            vg = dot(probs, ag, TN).astype(BF16)
            qg = dot(sg, k).astype(BF16)
            kg = dot(sg, q, TN).astype(BF16)
            for i, (g, f) in enumerate(((qg, qf), (kg, kf), (vg, vf))):
                grads[i].append(g)
                g32 = g.astype(F32)
                u = jnp.sum(acc[i, ROWS:, cols], axis=0, keepdims=True)
                s1 = s1 + jnp.sum(g32 * u, axis=1, keepdims=True)
                s2 = s2 + jnp.sum(g32 * f, axis=1, keepdims=True)
        attn_rows.append(jnp.concatenate(attn, axis=1))
        grad_rows.append([jnp.concatenate(g, axis=1) for g in grads])
        s1_rows.append(s1)
        s2_rows.append(s2)
    attn = jnp.concatenate(attn_rows, axis=0)
    grads = [jnp.concatenate([g[i] for g in grad_rows], axis=0) for i in range(3)]

    sib_nd = {}
    for xx in range(NX):
        for cc in range(2):
            t = xx * 2 + cc
            wts = [wbuf[i, t * W : t * W + W] for i in range(3)]
            p = dot(grads[0], wts[0], NT) + dot(grads[1], wts[1], NT) + dot(grads[2], wts[2], NT)
            for n in range(3):
                part_n[cc, xx, n] = p[:, n * 128 : n * 128 + 128].astype(BF16)
        sib_nd[xx] = copy(part_n.at[oc, xx], sib_n.at[xx], S_NS + xx, (dp, tens(0, oc)))
    s1r = jnp.sum(jnp.where(eye, jnp.concatenate(s1_rows, axis=0), 0.0), axis=0, keepdims=True)
    s2r = jnp.sum(jnp.where(eye, jnp.concatenate(s2_rows, axis=0), 0.0), axis=0, keepdims=True)
    scal[tn] = jnp.concatenate([s1r, s2r, jnp.zeros((6, ROWS), F32)], axis=0)
    own_s = scal.at[tn]
    sc_d = [copy(own_s, own_s, S_SC + k - 1, (dp, tens(k, c))) for k in (1, 2, 3)]
    sc_d += [copy(own_s, own_s, S_SC + 3 + k, (dp, tens(k, oc))) for k in range(4)]
    for t in range(8):
        part_o[t % 2, t // 2] = dot(attn, wbuf[3, t * W : t * W + W], NT).astype(BF16)
    sib_od = copy(part_o.at[oc], sib_o, S_OS, (dp, tens(0, oc)))

    for xx in range(NX):
        sib_nd[xx].wait_recv()
    rs_n = {}
    for n in range(3):
        for k in (2, 1, 3):
            xx = lax.rem(x + k, NX)
            q_n[xx, n] = (part_n[c, xx, n].astype(F32) + sib_n[xx, n].astype(F32)).astype(BF16)
            rs_n[n, k] = copy(
                q_n.at[xx, n], rx_n.at[k - 1, n], S_NX + n * 3 + k - 1, (dp, tens(k, c))
            )

    local = xg[tn].astype(F32)
    unit = (local - mean) * inv_std
    for d in sc_d:
        d.wait_recv()
    sums = scal[0]
    for t in range(1, 8):
        sums = sums + scal[t]
    mean1 = jnp.sum(jnp.where(eye, sums[0:1, :], 0.0), axis=1, keepdims=True) * (1.0 / D)
    mean2 = jnp.sum(jnp.where(eye, sums[1:2, :], 0.0), axis=1, keepdims=True) * (1.0 / D)

    r1, r2, rs_o = {}, {}, {}

    def return_y(n):
        lanes = slice(n * 128, n * 128 + 128)
        ng = part_n[c, x, n].astype(F32) + sib_n[x, n].astype(F32)
        for k in (1, 2, 3):
            rs_n[n, k].wait_recv()
            ng = ng + rx_n[k - 1, n].astype(F32)
        back = inv_std * (ng * gain_ref[tn][:, lanes] - mean1 - unit[:, lanes] * mean2)
        moved = jnp.where(live, cot_ref[:, lanes].astype(F32) + back, 0.0).astype(BF16)
        ret1[n] = dot(pick_t[...], moved).astype(BF16).reshape(NY, 128, 128)
        for k in (1, 2, 3):
            p = lax.rem(y + k, NY)
            r1[n, k] = copy(ret1.at[n, p], got1.at[n, y], S_R1 + n * 3 + k - 1, (at(0, k), tn))
        got1[n, y] = ret1[n, y]

    def return_z(n):
        for k in (1, 2, 3):
            r1[n, k].wait_recv()
        tiles = got1[n].astype(F32)
        for s in range(NZ):
            ret2[n, s] = jnp.concatenate(
                [tiles[q, s * 8 : s * 8 + 8, :] for q in range(NY)], axis=0
            ).astype(BF16)
        for k in (8, 7, 9, 6, 10, 5, 11, 4, 12, 3, 13, 2, 14, 1, 15):
            p = lax.rem(z + k, NZ)
            r2[n, k] = copy(ret2.at[n, p], got2.at[n, z], S_R2 + n * 15 + k - 1, (at(k), tn))
        got2[n, z] = ret2[n, z]

    def return_last(n):
        for k in range(1, NZ):
            r2[n, k].wait_recv()
        pg_ref[:, n * 128 : n * 128 + 128] = dot(
            pack_t[...], got2[n].reshape(512, 128)
        ).astype(BF16)

    return_y(0)
    return_y(1)
    return_z(0)
    return_y(2)
    return_z(1)
    sib_od.wait_recv()
    for k in (2, 1, 3):
        xx = lax.rem(x + k, NX)
        q_o[xx] = (part_o[c, xx].astype(F32) + sib_o[xx].astype(F32)).astype(BF16)
        rs_o[k] = copy(q_o.at[xx], rx_o.at[k - 1], S_OX + k - 1, (dp, tens(k, c)))
    return_z(2)
    branch = part_o[c, x].astype(F32) + sib_o[x].astype(F32)
    for k in (1, 2, 3):
        rs_o[k].wait_recv()
        branch = branch + rx_o[k - 1].astype(F32)
    mixed_ref[...] = jnp.where(live, local + branch, 0.0).astype(BF16)
    for n in range(3):
        return_last(n)
    for d in pending:
        d.wait_send()


def per_device(patches, counts, target, ln_gain, w_qkv, w_out, cotangent):
    images, slot_len, width = patches.shape
    pos = jnp.arange(slot_len, dtype=jnp.int32)[None, :]
    dest = (target[:, None] * slot_len + pos).reshape(1, ROWS)
    ids = jnp.arange(images, dtype=jnp.int32)[:, None] * slot_len + pos
    slot = jnp.where(pos < counts[:, None], ids, -1).reshape(1, ROWS)
    meta = jnp.concatenate([dest, slot, jnp.zeros((6, ROWS), jnp.int32)], axis=0)
    vm = pl.BlockSpec(memory_space=pltpu.VMEM)
    b = lambda *s: pltpu.VMEM(s, BF16)
    f = lambda *s: pltpu.VMEM(s, F32)
    scratch = [
        b(4, D, W), b(8, ROWS, W), b(8, ROWS, W), b(NZ, ROWS + 16, SLAB), b(NZ, ROWS, SLAB),
        b(NZ, 32, W), b(NZ, 32, W), b(NY, 128, W), b(NY, 128, W),
        f(NZ, 1, 128), f(NZ, 1, 128), f(NY, NZ, 1, 128),
        b(ROWS, 512), b(512, ROWS), b(ROWS, 512), f(4, ROWS + 16, W),
        b(2, 4, 3, ROWS, 128), b(2, 4, ROWS, W), b(4, 3, ROWS, 128), b(4, ROWS, W),
        b(4, 3, ROWS, 128), b(4, ROWS, W), b(3, 3, ROWS, 128), b(3, ROWS, W), f(8, 8, ROWS),
        b(3, NY, 128, 128), b(3, NY, 128, 128), b(3, NZ, 32, 128), b(3, NZ, 32, 128),
        pltpu.SemaphoreType.DMA((N_SEM,)), pltpu.SemaphoreType.DMA((N_SEM,)),
    ]
    mixed, grad = pl.pallas_call(
        block_kernel,
        out_shape=[jax.ShapeDtypeStruct((ROWS, W), BF16)] * 2,
        in_specs=[vm] * 6,
        out_specs=[vm] * 2,
        scratch_shapes=scratch,
        compiler_params=pltpu.CompilerParams(
            collective_id=0, has_side_effects=True, vmem_limit_bytes=56 << 20
        ),
        name="attention_block",
    )(
        meta, patches.reshape(ROWS, width), cotangent.reshape(ROWS, width),
        ln_gain.reshape(8, 1, W), w_qkv, w_out.T,
    )
    return mixed.reshape(patches.shape), grad.reshape(patches.shape)


def solution(mesh):
    in_specs = (
        P("dp", None, "tensor"), P("dp"), P("dp"), P(), P(None, "dp", "tensor"),
        P("tensor", "dp"), P("dp", None, "tensor"),
    )
    out_specs = (P("dp", None, "tensor"), P("dp", None, "tensor"))
    return jax.shard_map(
        per_device, mesh=mesh, in_specs=in_specs, out_specs=out_specs, check_vma=False
    )
```

time: 162 us -> 147 us (0.907)
  Pallas kernels: 156 us -> 140 us
    pallas_call x1, Pallas kernels: 156 us -> 140 us  [per_device(): pl.pallas_call(block_kernel, out_shape=[jax.ShapeDtypeStruct((ROWS, W), B...]
where the time goes in v2:
time: 147 us; the launch traced here: 145 us
  Pallas kernels  140 us (95%)
  local copies, waits for them, and re-layouts  3.9 us (3%)
    pallas_call x1, Pallas kernels, per_device(): pl.pallas_call(block_kernel, out_shape=[jax.ShapeDtypeStruct((ROWS, W), B...  140 us
    unnamed x8, local copies, waits for them, and re-layouts  3.64 us

profile of v2, /device:TPU:1, one launch (start us, length us, event | category | flops | bytes accessed | tf_op | source)
XLA Modules:
  0.0 145.2 jit_solution(850064535674560301)
XLA Ops:
  0.6 0.0 copy-start.2
  0.6 0.6 copy-done.2
  1.3 0.1 pad.2.clone
  1.4 0.0 copy-start.1
  1.4 0.6 copy-done.1
  2.0 0.1 add_select_fusion
  2.1 0.1 select_n.15
  2.2 0.1 iota_add_fusion
  2.3 0.1 add.49
  2.4 0.7 add_add_fusion.meta_ref
  3.0 139.8 %attention_block.1 = (bf16[256,384]{1,0:T(8,128)(2,1)}, bf16[256,384]{1,0:T(8,128)(2,1)}) custom-call(s32[8,256]{1,0:T(8,128)} %add_add_fusion.meta_ref, bf16[256,384]{1,0:T(8,128)(2,1)} %bitcast.6, bf16[256,384]{1,0:T(8,128)(2,1)} %bitcast.7, f32[8,1,384]{2,1,0:T(1,128)} %bitcast.11, bf16[3,48,384]{2,1,0:T(8,128)(2,1)} %wqkv_ref.1, bf16[48,384]{1,0:T(8,128)(2,1)} %bitcast.10), custom_call_target="tpu_custom_call" | custom-call | tf_op jit(solution)/shard_map/attention_block/pallas_call | solution.py:537
  142.9 0.0 copy-start
  142.9 1.7 %copy.11 = bf16[32,8,384]{2,1,0:T(8,128)(2,1)} copy(bf16[32,8,384]{2,1,0:T(8,128)(2,1)} %bitcast.9) | data formatting | bytes 393216
  144.5 0.0 copy-done
  144.5 0.7 copy.12
  (3 shorter events, 0.0 us)
Async XLA Ops:
  0.6 0.7 copy-start.2
  1.4 0.7 copy-start.1
  142.9 1.7 %copy-start = (bf16[256,384]{1,0:T(8,128)(2,1)S(1)}, bf16[256,384]{1,0:T(8,128)(2,1)}, u32[]{:S(2)}) copy-start(bf16[256,384]{1,0:T(8,128)(2,1)} %get-tuple-element.5) | copy-start | bytes 589828

commit v3 on v2

v3 whole, which is shorter than its diff:
```python
import jax
import jax.numpy as jnp
from jax import lax
from jax.experimental import pallas as pl
from jax.experimental.pallas import tpu as pltpu
from jax.sharding import PartitionSpec as P

HD = 128
D = 3072
NZ, NY, NX = 16, 4, 4
ROWS = 256
W = 384
SHARD = 48
SLAB = 192
F32 = jnp.float32
BF16 = jnp.bfloat16
NT = (((1,), (1,)), ((), ()))
TN = (((0,), (0,)), ((), ()))
S_COT = 0
S_XG = 7
S_A1 = 14
S_M1 = 17
S_A2 = 20
S_M2 = 35
S_AY = 50
S_AZR = 53
S_AZL = 61
S_BZR = 68
S_BZL = 76
S_BYR = 83
S_BYL = 99
S_BREL = 115
S_NS = 131
S_NX = 134
S_OS = 143
S_OX = 144
S_SC = 147
S_R1 = 154
S_R2 = 199
N_SEM = 208


def dot(a, b, dims=(((1,), (0,)), ((), ()))):
    return lax.dot_general(a, b, dims, preferred_element_type=F32)


def block_kernel(
    target_ref, counts_ref, x_hbm, cot_hbm, gain_hbm, wqkv_hbm, wout_hbm, mixed_ref, pg_ref,
    x_ref, cot_ref, gain_ref, wbuf, xg, cg, nb, gb, send, mid, mid2, recv, msend, mrecv, mall,
    pick, pick_t, pack_t, acc, part_n, part_o, sib_n, sib_o, q_n, q_o, rx_n, rx_o, scal,
    ret1, got1, ret2, got2, ssem, rsem, lsem,
):
    dp = lax.axis_index("dp")
    tn = lax.axis_index("tensor")
    z, y = lax.div(dp, NY), lax.rem(dp, NY)
    x, c = lax.div(tn, 2), lax.rem(tn, 2)
    oc = 1 - c

    def at(dz=0, dy=0):
        return lax.rem(z + dz + NZ, NZ) * NY + lax.rem(y + dy + NY, NY)

    def tens(dx, core):
        return lax.rem(x + dx, NX) * 2 + core

    def rows_of(p):
        return pl.ds(pl.multiple_of(p * SHARD, SHARD), SHARD)

    def slab(zz):
        return pl.ds(pl.multiple_of(zz * SLAB, SLAB), SLAB)

    barrier = pltpu.get_barrier_semaphore()
    peers = [(at(k, 0), tn) for k in range(1, NZ)]
    peers += [(at(0, k), tn) for k in range(1, NY)]
    peers += [(dp, tens(k, c)) for k in range(1, NX)]
    peers += [(dp, tens(k, oc)) for k in range(NX)]
    for peer in peers:
        pl.semaphore_signal(barrier, inc=1, device_id=peer, device_id_type=pl.DeviceIdType.MESH)
    loads = []
    for i, (a, b) in enumerate((
        (wqkv_hbm, wbuf.at[pl.ds(0, 3), rows_of(dp)]), (wout_hbm, wbuf.at[3, rows_of(dp)]),
        (cot_hbm, cg.at[tn]), (x_hbm, x_ref), (cot_hbm, cot_ref), (gain_hbm, gain_ref),
    )):
        loads.append(pltpu.make_async_copy(a, b, lsem.at[i]))
        loads[-1].start()

    pending = []

    def copy(src, dst, sem, to):
        desc = pltpu.make_async_remote_copy(
            src_ref=src, dst_ref=dst, send_sem=ssem.at[sem], recv_sem=rsem.at[sem],
            device_id=to, device_id_type=pl.DeviceIdType.MESH,
        )
        desc.start()
        pending.append(desc)
        return desc

    eye = lax.broadcasted_iota(jnp.int32, (ROWS, ROWS), 0) == lax.broadcasted_iota(
        jnp.int32, (ROWS, ROWS), 1
    )
    for d in loads:
        d.wait()
    pl.semaphore_wait(barrier, len(peers))

    def b_zr(j):
        r = wbuf.at[pl.ds(0, 3), rows_of(at(-j))]
        return copy(r, r, S_BZR + j, (at(1), tn))

    def b_zl(j):
        r = wbuf.at[pl.ds(0, 3), rows_of(at(j))]
        return copy(r, r, S_BZL + j, (at(-1), tn))

    def b_y(d):
        r = wbuf.at[pl.ds(0, 3), rows_of(at(d))]
        return copy(r, r, S_BYR + d, (at(0, 1), tn)), copy(r, r, S_BYL + d, (at(0, -1), tn))

    def b_relay(d, up):
        r = wbuf.at[pl.ds(0, 3), rows_of(at(d, -1 if up else 1))]
        return copy(r, r, S_BREL + d, (at(0, 1 if up else -1), tn))

    def a_zr(j):
        r = wbuf.at[3, slab(lax.rem(z - j + NZ, NZ))]
        return copy(r, r, S_AZR + j, (at(1), tn))

    def a_zl(j):
        r = wbuf.at[3, slab(lax.rem(z + j, NZ))]
        return copy(r, r, S_AZL + j, (at(-1), tn))

    zr, zl, yy, rel, azr, azl = {}, {}, {}, {}, {}, {}
    a_y, a1, m1, a2, m2, cot_d, cot_f, xg_d, xg_f = [], [], [], [], [], [], [], [], []

    def tiles_sort():
        spread = (
            lax.shift_right_logical(lax.broadcasted_iota(jnp.int32, (32, ROWS), 1), 3)
            == lax.broadcasted_iota(jnp.int32, (32, ROWS), 0)
        ).astype(BF16)
        pair = jnp.concatenate(
            [target_ref[...].astype(F32), counts_ref[...].astype(F32), jnp.zeros((14, 32), F32)],
            axis=0,
        ).astype(BF16)
        pair = dot(pair, spread).astype(jnp.int32)
        lane = lax.broadcasted_iota(jnp.int32, (1, ROWS), 1)
        row = lax.bitwise_and(lane, 7)
        to = pair[0:1, :]
        dest = lax.bitwise_and(to, 3) * 128 + lax.shift_right_logical(to, 2) * 8 + row
        slot = jnp.where(row < pair[1:2, :], lane, -1)
        pack = (lax.broadcasted_iota(jnp.int32, (512, ROWS), 0) == dest).astype(BF16)
        send[...] = dot(pack, x_ref[...]).astype(BF16).reshape(NY, 128, W)
        a_meta = jnp.where(
            lax.broadcasted_iota(jnp.int32, (16, ROWS), 0) == lax.shift_right_logical(dest, 7),
            slot + 1, 0,
        ).astype(F32).astype(BF16)
        b_meta = (
            lax.broadcasted_iota(jnp.int32, (128, ROWS), 0) == lax.bitwise_and(dest, 127)
        ).astype(BF16)
        meta_rows = dot(a_meta, b_meta, NT)
        for k in range(NY):
            msend[k] = meta_rows[k : k + 1, :]
        for k in (1, 2, 3):
            p = lax.rem(y + k, NY)
            m1.append(copy(msend.at[p], mrecv.at[y], S_M1 + k - 1, (at(0, k), tn)))
            a1.append(copy(send.at[p], mid.at[y], S_A1 + k - 1, (at(0, k), tn)))
        mid[y] = send[y]
        mrecv[y] = msend[y]
        pack_t[...] = dot(eye.astype(BF16), pack, NT).astype(BF16)

    def tiles_second():
        for d in a1 + m1:
            d.wait_recv()
        tiles = mid[...].astype(F32)
        for q in range(NZ):
            mid2[q] = jnp.concatenate(
                [tiles[s, q * 8 : q * 8 + 8, :] for s in range(NY)], axis=0
            ).astype(BF16)
        recv[z] = mid2[z]
        mall[z] = mrecv[...]

    def tiles_z(*ks):
        for k in ks:
            p = lax.rem(z + k, NZ)
            m2.append(copy(mrecv, mall.at[z], S_M2 + k - 1, (at(k), tn)))
            a2.append(copy(mid2.at[p], recv.at[z], S_A2 + k - 1, (at(k), tn)))

    def tiles_last():
        for d in a2 + m2:
            d.wait_recv()
        lane = lax.broadcasted_iota(jnp.int32, (128, 512), 1)
        sel = (
            lax.broadcasted_iota(jnp.int32, (128, 512), 0) == z * 8 + lax.bitwise_and(lane, 7)
        ).astype(BF16)
        mine = (
            lax.broadcasted_iota(jnp.int32, (64, 512), 0)
            == lax.shift_right_logical(lax.broadcasted_iota(jnp.int32, (64, 512), 1), 3)
        )
        rows = jnp.concatenate([mall[q, s] for q in range(NZ) for s in range(NY)], axis=0)
        where_to = jnp.sum(
            jnp.where(mine, dot(rows.astype(BF16), sel), 0.0), axis=0, keepdims=True
        ).astype(jnp.int32) - 1
        picked = (lax.broadcasted_iota(jnp.int32, (ROWS, 512), 0) == where_to).astype(BF16)
        pick[...] = picked
        xg[tn] = dot(picked, recv[...].reshape(512, W)).astype(BF16)
        xg_d.extend(gather_start(xg, S_XG))

    def tiles_after():
        eye512 = lax.broadcasted_iota(jnp.int32, (512, 512), 0) == lax.broadcasted_iota(
            jnp.int32, (512, 512), 1
        )
        pick_t[...] = dot(eye512.astype(BF16), pick[...], NT).astype(BF16)
        live_col = jnp.sum(pick[...].astype(F32), axis=1, keepdims=True)
        st["live_row"] = jnp.sum(jnp.where(eye, live_col, 0.0), axis=0, keepdims=True)
        st["live"] = live_col > 0.5

    def gather_start(buf, base):
        own = buf.at[tn]
        sib = copy(own, own, base, (dp, tens(0, oc)))
        return [sib] + [copy(own, own, base + k, (dp, tens(k, c))) for k in (1, 2, 3)]

    def gather_pass(buf, base, ds):
        out = []
        for k in (1, 2, 3):
            ds[k].wait_recv()
            r = buf.at[tens(NX - k, c)]
            out.append(copy(r, r, base + 3 + k, (dp, tens(0, oc))))
        return out

    def a_first():
        for k in (1, 2, 3):
            r = wbuf.at[3, rows_of(dp)]
            a_y.append(copy(r, r, S_AY + k - 1, (at(0, k), tn)))

    def b_step(j):
        if j == 0:
            zr[0], zl[0] = b_zr(0), b_zl(0)
            yy[0] = b_y(0)
            return
        zr[j - 1].wait_recv()
        if j < 8:
            zr[j] = b_zr(j)
        yy[NZ - j] = b_y(NZ - j)
        if j < 8:
            zl[j - 1].wait_recv()
            if j < 7:
                zl[j] = b_zl(j)
            yy[j] = b_y(j)

    def relay_step(j):
        if j > 0:
            d = NZ - j
            yy[d][0].wait_recv()
            rel[d] = b_relay(d, True)
        if j < 8:
            yy[j][1].wait_recv()
            rel[j] = b_relay(j, False)

    def a_step(j):
        if j == 0:
            for d in a_y:
                d.wait_recv()
        else:
            azr[j - 1].wait_recv()
            if j < 8:
                azl[j - 1].wait_recv()
        if j < 8:
            azr[j] = a_zr(j)
        if j < 7:
            azl[j] = a_zl(j)

    def b_done(j):
        d = (NZ - j) % NZ
        if j > 0:
            yy[d][1].wait_recv()
            rel[d].wait_recv()
        if j < 8:
            yy[j][0].wait_recv()
            rel[j].wait_recv()

    def project_qkv(j):
        b_done(j)
        for zz in {0: (z,), 8: (lax.rem(z + 8, NZ),)}.get(
            j, (lax.rem(z + j, NZ), lax.rem(z - j + NZ, NZ))
        ):
            rows = nb[zz]
            for i in range(3):
                p = dot(rows, wbuf[i, slab(zz)])
                acc[i] = p if j == 0 else acc[i] + p

    def project_grad(j):
        for zz in {0: (z,), 8: (lax.rem(z + 8, NZ),)}.get(
            j, (lax.rem(z + j, NZ), lax.rem(z - j + NZ, NZ))
        ):
            p = dot(gb[zz], wbuf[3, slab(zz)])
            acc[3, 0:ROWS] = p if j == 0 else acc[3, 0:ROWS] + p

    def grads_ready():
        cot_d[0].wait_recv()
        for d in cot_f:
            d.wait_recv()
        for t in range(8):
            g = jnp.where(st["live"], cg[t], jnp.zeros((), BF16))
            gb[2 * t] = g[:, :SLAB]
            gb[2 * t + 1] = g[:, SLAB:]

    def norm():
        xg_d[0].wait_recv()
        for d in xg_f:
            d.wait_recv()
        total = jnp.zeros((ROWS, 1), F32)
        for t in range(8):
            total = total + jnp.sum(xg[t].astype(F32), axis=1, keepdims=True)
        mean = total * (1.0 / D)
        sq = jnp.zeros((ROWS, 1), F32)
        for t in range(8):
            cen = xg[t].astype(F32) - mean
            sq = sq + jnp.sum(cen * cen, axis=1, keepdims=True)
        inv_std = lax.rsqrt(sq * (1.0 / D) + 1e-06)
        for t in range(8):
            gain = gain_ref[t]
            normed = ((xg[t].astype(F32) - mean) * inv_std * gain).astype(BF16)
            g0 = gain.astype(BF16).astype(F32)
            g1 = (gain - g0).astype(BF16).astype(F32)
            g2 = (gain - g0 - g1).astype(BF16).astype(F32)
            gains = jnp.concatenate([g0, g1, g2, jnp.zeros((13, W), F32)], axis=0).astype(BF16)
            for half in range(2):
                lanes = slice(half * SLAB, (half + 1) * SLAB)
                nb[2 * t + half, 0:ROWS] = normed[:, lanes]
                nb[2 * t + half, ROWS:] = gains[:, lanes]
        st["mean"], st["inv_std"] = mean, inv_std

    st = {}

    def cot_start():
        cot_d.extend(gather_start(cg, S_COT))

    def cot_pass():
        cot_f.extend(gather_pass(cg, S_COT, cot_d))

    def x_pass():
        xg_f.extend(gather_pass(xg, S_XG, xg_d))

    b_step(0)
    a_first()
    cot_start()
    tiles_sort()
    b_step(1)
    relay_step(0)
    tiles_second()
    tiles_z(8,7,9,6,10)
    b_step(2)
    tiles_z(5,11,4,12,3)
    relay_step(1)
    a_step(0)
    b_step(3)
    tiles_z(13,2,14,1,15)
    relay_step(2)
    a_step(1)
    b_step(4)
    cot_pass()
    relay_step(3)
    a_step(2)
    b_step(5)
    relay_step(4)
    a_step(3)
    tiles_last()
    tiles_after()
    b_step(6)
    relay_step(5)
    a_step(4)
    b_step(7)
    grads_ready()
    relay_step(6)
    a_step(5)
    x_pass()
    b_step(8)
    norm()
    relay_step(7)
    a_step(6)
    project_qkv(0)
    project_qkv(1)
    relay_step(8)
    project_qkv(2)
    a_step(7)
    project_qkv(3)
    project_qkv(4)
    a_step(8)
    project_qkv(5)
    project_qkv(6)
    for j in range(9):
        project_grad(j)
    project_qkv(7)
    project_qkv(8)
    live, live_row, mean, inv_std = st["live"], st["live_row"], st["mean"], st["inv_std"]

    half_rows = ROWS // 2
    row_img = lax.shift_right_logical(
        lax.broadcasted_iota(jnp.int32, (half_rows, half_rows), 0), 3
    )
    col_img = lax.shift_right_logical(
        lax.broadcasted_iota(jnp.int32, (half_rows, half_rows), 1), 3
    )
    same = row_img == col_img
    scale = HD ** (-0.5)
    blocks = [
        (slice(r * half_rows, (r + 1) * half_rows), slice(h * HD, (h + 1) * HD))
        for r in range(2) for h in range(3)
    ]
    qkv = [[acc[i, rs, cols].astype(BF16) for i in range(3)] for rs, cols in blocks]
    ag = [acc[3, rs, cols].astype(BF16) for rs, cols in blocks]
    ok = [same & (live_row[:, rs] > 0.5) for rs, _ in blocks]
    sc = [jnp.where(m, dot(q, k, NT) * scale, -1e30) for m, (q, k, v) in zip(ok, qkv)]
    dprobs = [dot(a, v, NT) for a, (q, k, v) in zip(ag, qkv)]
    ex = [jnp.exp(a - jnp.max(a, axis=1, keepdims=True)) for a in sc]
    probs = [(a / jnp.sum(a, axis=1, keepdims=True)).astype(BF16) for a in ex]
    attn = [dot(p, v).astype(BF16) for p, (q, k, v) in zip(probs, qkv)]
    probs32 = [p.astype(F32) for p in probs]
    inner = [jnp.sum(d * p, axis=1, keepdims=True) for d, p in zip(dprobs, probs32)]
    sg = [(p * (d - n) * scale).astype(BF16) for p, d, n in zip(probs32, dprobs, inner)]
    vg = [dot(p, a, TN).astype(BF16) for p, a in zip(probs, ag)]
    qg = [dot(a, k).astype(BF16) for a, (q, k, v) in zip(sg, qkv)]
    kg = [dot(a, q, TN).astype(BF16) for a, (q, k, v) in zip(sg, qkv)]

    def whole(parts):
        return jnp.concatenate(
            [jnp.concatenate(parts[r * 3 : r * 3 + 3], axis=1) for r in range(2)], axis=0
        )

    grads = [whole(g) for g in (qg, kg, vg)]

    sib_nd, rs_n, sc_d = [], {}, []

    def partial(n):
        for t in range(8):
            rows = slice(t * W + n * 128, t * W + n * 128 + 128)
            p = dot(grads[0], wbuf[0, rows], NT)
            p = p + dot(grads[1], wbuf[1, rows], NT) + dot(grads[2], wbuf[2, rows], NT)
            part_n[t % 2, n, t // 2] = p.astype(BF16)
        sib_nd.append(copy(part_n.at[oc, n], sib_n.at[n], S_NS + n, (dp, tens(0, oc))))

    def fold(n):
        sib_nd[n].wait_recv()
        for k in (2, 1, 3):
            xx = lax.rem(x + k, NX)
            q_n[n, xx] = (part_n[c, n, xx].astype(F32) + sib_n[n, xx].astype(F32)).astype(BF16)
            rs_n[n, k] = copy(
                q_n.at[n, xx], rx_n.at[n, k - 1], S_NX + n * 3 + k - 1, (dp, tens(k, c))
            )

    def row_sums():
        s1, s2 = [], []
        for r in range(2):
            rs = slice(r * half_rows, (r + 1) * half_rows)
            a1s = jnp.zeros((half_rows, HD), F32)
            a2s = jnp.zeros((half_rows, HD), F32)
            for h in range(3):
                cols = slice(h * HD, (h + 1) * HD)
                for i, g in enumerate((qg, kg, vg)):
                    g32 = g[r * 3 + h].astype(F32)
                    a1s = a1s + g32 * jnp.sum(acc[i, ROWS:, cols], axis=0, keepdims=True)
                    a2s = a2s + g32 * acc[i, rs, cols]
            s1.append(jnp.sum(a1s, axis=1, keepdims=True))
            s2.append(jnp.sum(a2s, axis=1, keepdims=True))
        s1r = jnp.sum(jnp.where(eye, jnp.concatenate(s1, axis=0), 0.0), axis=0, keepdims=True)
        s2r = jnp.sum(jnp.where(eye, jnp.concatenate(s2, axis=0), 0.0), axis=0, keepdims=True)
        scal[tn] = jnp.concatenate([s1r, s2r, jnp.zeros((6, ROWS), F32)], axis=0)
        own_s = scal.at[tn]
        sc_d.extend([copy(own_s, own_s, S_SC + k - 1, (dp, tens(k, c))) for k in (1, 2, 3)])
        sc_d.extend([copy(own_s, own_s, S_SC + 3 + k, (dp, tens(k, oc))) for k in range(4)])

    partial(0)
    row_sums()
    partial(1)
    fold(0)
    partial(2)
    fold(1)
    fold(2)
    local = xg[tn].astype(F32)
    unit = (local - mean) * inv_std
    for d in sc_d:
        d.wait_recv()
    sums = scal[0]
    for t in range(1, 8):
        sums = sums + scal[t]
    mean1 = jnp.sum(jnp.where(eye, sums[0:1, :], 0.0), axis=1, keepdims=True) * (1.0 / D)
    mean2 = jnp.sum(jnp.where(eye, sums[1:2, :], 0.0), axis=1, keepdims=True) * (1.0 / D)

    r1, r2, rs_o = {}, {}, {}

    def return_z(n):
        lanes = slice(n * 128, n * 128 + 128)
        ng = part_n[c, n, x].astype(F32) + sib_n[n, x].astype(F32)
        for k in (1, 2, 3):
            rs_n[n, k].wait_recv()
            ng = ng + rx_n[n, k - 1].astype(F32)
        back = inv_std * (ng * gain_ref[tn][:, lanes] - mean1 - unit[:, lanes] * mean2)
        moved = jnp.where(live, cot_ref[:, lanes].astype(F32) + back, 0.0).astype(BF16)
        ret1[n] = dot(pick_t[...], moved).astype(BF16).reshape(NZ, 32, 128)
        for k in (8, 7, 9, 6, 10, 5, 11, 4, 12, 3, 13, 2, 14, 1, 15):
            p = lax.rem(z + k, NZ)
            r1[n, k] = copy(ret1.at[n, p], got1.at[n, z], S_R1 + n * 15 + k - 1, (at(k), tn))
        got1[n, z] = ret1[n, z]

    def return_y(n):
        for k in range(1, NZ):
            r1[n, k].wait_recv()
        tiles = got1[n].astype(F32)
        for q in range(NY):
            ret2[n, q] = jnp.concatenate(
                [tiles[s, q * 8 : q * 8 + 8, :] for s in range(NZ)], axis=0
            ).astype(BF16)
        for k in (1, 2, 3):
            p = lax.rem(y + k, NY)
            r2[n, k] = copy(ret2.at[n, p], got2.at[n, y], S_R2 + n * 3 + k - 1, (at(0, k), tn))
        got2[n, y] = ret2[n, y]

    def return_last(n):
        for k in (1, 2, 3):
            r2[n, k].wait_recv()
        pg_ref[:, n * 128 : n * 128 + 128] = dot(
            pack_t[...], got2[n].reshape(512, 128)
        ).astype(BF16)

    return_z(0)
    attn_all = whole(attn)
    for t in range(8):
        part_o[t % 2, t // 2] = dot(attn_all, wbuf[3, t * W : t * W + W], NT).astype(BF16)
    sib_od = copy(part_o.at[oc], sib_o, S_OS, (dp, tens(0, oc)))
    return_z(1)
    return_z(2)
    sib_od.wait_recv()
    for k in (2, 1, 3):
        xx = lax.rem(x + k, NX)
        q_o[xx] = (part_o[c, xx].astype(F32) + sib_o[xx].astype(F32)).astype(BF16)
        rs_o[k] = copy(q_o.at[xx], rx_o.at[k - 1], S_OX + k - 1, (dp, tens(k, c)))
    return_y(0)
    return_y(1)
    branch = part_o[c, x].astype(F32) + sib_o[x].astype(F32)
    for k in (1, 2, 3):
        rs_o[k].wait_recv()
        branch = branch + rx_o[k - 1].astype(F32)
    mixed_ref[...] = jnp.where(live, local + branch, 0.0).astype(BF16)
    return_last(0)
    return_y(2)
    return_last(1)
    return_last(2)
    for d in pending:
        d.wait_send()


def per_device(patches, counts, target, ln_gain, w_qkv, w_out, cotangent):
    images, slot_len, width = patches.shape
    vm = pl.BlockSpec(memory_space=pltpu.VMEM)
    b = lambda *s: pltpu.VMEM(s, BF16)
    f = lambda *s: pltpu.VMEM(s, F32)
    scratch = [
        b(ROWS, W), b(ROWS, W), f(8, 1, W),
        b(4, D, W), b(8, ROWS, W), b(8, ROWS, W), b(NZ, ROWS + 16, SLAB), b(NZ, ROWS, SLAB),
        b(NY, 128, W), b(NY, 128, W), b(NZ, 32, W), b(NZ, 32, W),
        f(NY, 1, 128), f(NY, 1, 128), f(NZ, NY, 1, 128),
        b(ROWS, 512), b(512, ROWS), b(ROWS, 512), f(4, ROWS + 16, W),
        b(2, 3, 4, ROWS, 128), b(2, 4, ROWS, W), b(3, 4, ROWS, 128), b(4, ROWS, W),
        b(3, 4, ROWS, 128), b(4, ROWS, W), b(3, 3, ROWS, 128), b(3, ROWS, W), f(8, 8, ROWS),
        b(3, NZ, 32, 128), b(3, NZ, 32, 128), b(3, NY, 128, 128), b(3, NY, 128, 128),
        pltpu.SemaphoreType.DMA((N_SEM,)), pltpu.SemaphoreType.DMA((N_SEM,)),
        pltpu.SemaphoreType.DMA((6,)),
    ]
    mixed, grad = pl.pallas_call(
        block_kernel,
        out_shape=[jax.ShapeDtypeStruct((ROWS, W), BF16)] * 2,
        in_specs=[vm] * 2 + [pl.BlockSpec(memory_space=pl.ANY)] * 5,
        out_specs=[vm] * 2,
        scratch_shapes=scratch,
        compiler_params=pltpu.CompilerParams(
            collective_id=0, has_side_effects=True, vmem_limit_bytes=56 << 20
        ),
        name="attention_block",
    )(
        target.reshape(1, images), counts.reshape(1, images), patches.reshape(ROWS, width),
        cotangent.reshape(ROWS, width), ln_gain.reshape(8, 1, W), w_qkv, w_out.T,
    )
    return mixed.reshape(patches.shape), grad.reshape(patches.shape)


def solution(mesh):
    in_specs = (
        P("dp", None, "tensor"), P("dp"), P("dp"), P(), P(None, "dp", "tensor"),
        P("tensor", "dp"), P("dp", None, "tensor"),
    )
    out_specs = (P("dp", None, "tensor"), P("dp", None, "tensor"))
    return jax.shard_map(
        per_device, mesh=mesh, in_specs=in_specs, out_specs=out_specs, check_vma=False
    )
```

time: 147 us -> 139 us (0.946)
  Pallas kernels: 140 us -> 133 us
  local copies, waits for them, and re-layouts: 3.9 us -> 2.34 us
    pallas_call x1, Pallas kernels: 140 us -> 133 us  [per_device(): pl.pallas_call(block_kernel, out_shape=[jax.ShapeDtypeStruct((ROWS, W), B...]
    unnamed x8 -> x4, local copies, waits for them, and re-layouts: 3.64 us -> 2.34 us
where the time goes in v3:
time: 139 us; the launch traced here: 136 us
  Pallas kernels  133 us (96%)
  local copies, waits for them, and re-layouts  2.34 us (2%)
    pallas_call x1, Pallas kernels, per_device(): pl.pallas_call(block_kernel, out_shape=[jax.ShapeDtypeStruct((ROWS, W), B...  133 us

profile of v3, /device:TPU:1, one launch (start us, length us, event | category | flops | bytes accessed | tf_op | source)
XLA Modules:
  0.0 136.4 jit_solution(4352750777530870135)
XLA Ops:
  0.6 133.4 %attention_block.1 = (bf16[256,384]{1,0:T(8,128)(2,1)}, bf16[256,384]{1,0:T(8,128)(2,1)}) custom-call(s32[1,32]{1,0:T(1,128)} %bitcast.14, s32[1,32]{1,0:T(1,128)} %bitcast.15, bf16[256,384]{1,0:T(8,128)(2,1)} %bitcast.8, bf16[256,384]{1,0:T(8,128)(2,1)} %bitcast.9, f32[8,1,384]{2,1,0:T(1,128)} %bitcast.13, bf16[3,48,384]{2,1,0:T(8,128)(2,1)} %wqkv_hbm.1, ...), custom_call_target="tpu_custom_call" | custom-call | tf_op jit(solution)/shard_map/attention_block/pallas_call | solution.py:564
  134.0 0.0 copy-start
  134.0 1.7 %copy.11 = bf16[32,8,384]{2,1,0:T(8,128)(2,1)} copy(bf16[32,8,384]{2,1,0:T(8,128)(2,1)} %bitcast.11) | data formatting | bytes 393216
  135.7 0.0 copy-done
  135.7 0.7 copy.12
Async XLA Ops:
  134.0 1.7 %copy-start = (bf16[256,384]{1,0:T(8,128)(2,1)S(1)}, bf16[256,384]{1,0:T(8,128)(2,1)}, u32[]{:S(2)}) copy-start(bf16[256,384]{1,0:T(8,128)(2,1)} %get-tuple-element.5) | copy-start | bytes 589828

commit v4 on v3

--- a/solution.py
+++ b/solution.py
@@ -24,7 +24,7 @@
 S_M2 = 35
 S_AY = 50
 S_AZR = 53
-S_AZL = 61
+S_AZL = 60
 S_BZR = 68
 S_BZL = 76
 S_BYR = 83
@@ -97,36 +97,8 @@
     eye = lax.broadcasted_iota(jnp.int32, (ROWS, ROWS), 0) == lax.broadcasted_iota(
         jnp.int32, (ROWS, ROWS), 1
     )
-    for d in loads:
-        d.wait()
-    pl.semaphore_wait(barrier, len(peers))
-
-    def b_zr(j):
-        r = wbuf.at[pl.ds(0, 3), rows_of(at(-j))]
-        return copy(r, r, S_BZR + j, (at(1), tn))
-
-    def b_zl(j):
-        r = wbuf.at[pl.ds(0, 3), rows_of(at(j))]
-        return copy(r, r, S_BZL + j, (at(-1), tn))
-
-    def b_y(d):
-        r = wbuf.at[pl.ds(0, 3), rows_of(at(d))]
-        return copy(r, r, S_BYR + d, (at(0, 1), tn)), copy(r, r, S_BYL + d, (at(0, -1), tn))
-
-    def b_relay(d, up):
-        r = wbuf.at[pl.ds(0, 3), rows_of(at(d, -1 if up else 1))]
-        return copy(r, r, S_BREL + d, (at(0, 1 if up else -1), tn))
-
-    def a_zr(j):
-        r = wbuf.at[3, slab(lax.rem(z - j + NZ, NZ))]
-        return copy(r, r, S_AZR + j, (at(1), tn))
-
-    def a_zl(j):
-        r = wbuf.at[3, slab(lax.rem(z + j, NZ))]
-        return copy(r, r, S_AZL + j, (at(-1), tn))
-
-    zr, zl, yy, rel, azr, azl = {}, {}, {}, {}, {}, {}
-    a_y, a1, m1, a2, m2, cot_d, cot_f, xg_d, xg_f = [], [], [], [], [], [], [], [], []
+    st = {}
+    m1, a1 = [], []
 
     def tiles_sort():
         spread = (
@@ -155,13 +127,50 @@
         meta_rows = dot(a_meta, b_meta, NT)
         for k in range(NY):
             msend[k] = meta_rows[k : k + 1, :]
+        mid[y] = send[y]
+        mrecv[y] = msend[y]
+        st["dest"] = dest
+
+    def tiles_first():
         for k in (1, 2, 3):
             p = lax.rem(y + k, NY)
             m1.append(copy(msend.at[p], mrecv.at[y], S_M1 + k - 1, (at(0, k), tn)))
             a1.append(copy(send.at[p], mid.at[y], S_A1 + k - 1, (at(0, k), tn)))
-        mid[y] = send[y]
-        mrecv[y] = msend[y]
-        pack_t[...] = dot(eye.astype(BF16), pack, NT).astype(BF16)
+
+    def tiles_order():
+        pack = lax.broadcasted_iota(jnp.int32, (512, ROWS), 0) == st["dest"]
+        pack_t[...] = dot(eye.astype(BF16), pack.astype(BF16), NT).astype(BF16)
+
+    for d in loads:
+        d.wait()
+    pl.semaphore_wait(barrier, len(peers))
+
+    def b_zr(j):
+        r = wbuf.at[pl.ds(0, 3), rows_of(at(-j))]
+        return copy(r, r, S_BZR + j, (at(1), tn))
+
+    def b_zl(j):
+        r = wbuf.at[pl.ds(0, 3), rows_of(at(j))]
+        return copy(r, r, S_BZL + j, (at(-1), tn))
+
+    def b_y(d):
+        r = wbuf.at[pl.ds(0, 3), rows_of(at(d))]
+        return copy(r, r, S_BYR + d, (at(0, 1), tn)), copy(r, r, S_BYL + d, (at(0, -1), tn))
+
+    def b_relay(d, up):
+        r = wbuf.at[pl.ds(0, 3), rows_of(at(d, -1 if up else 1))]
+        return copy(r, r, S_BREL + d, (at(0, 1 if up else -1), tn))
+
+    def a_zr(j):
+        r = wbuf.at[3, slab(lax.rem(z - j + NZ, NZ))]
+        return copy(r, r, S_AZR + j, (at(1), tn))
+
+    def a_zl(j):
+        r = wbuf.at[3, slab(lax.rem(z + j, NZ))]
+        return copy(r, r, S_AZL + j, (at(-1), tn))
+
+    zr, zl, yy, rel, azr, azl = {}, {}, {}, {}, {}, {}
+    a_y, a2, m2, cot_d, cot_f, xg_d, xg_f = [], [], [], [], [], [], []
 
     def tiles_second():
         for d in a1 + m1:
@@ -256,13 +265,13 @@
             for d in a_y:
                 d.wait_recv()
         else:
-            azr[j - 1].wait_recv()
+            azl[j - 1].wait_recv()
             if j < 8:
-                azl[j - 1].wait_recv()
+                azr[j - 1].wait_recv()
         if j < 8:
+            azl[j] = a_zl(j)
+        if j < 7:
             azr[j] = a_zr(j)
-        if j < 7:
-            azl[j] = a_zl(j)
 
     def b_done(j):
         d = (NZ - j) % NZ
@@ -325,8 +334,6 @@
                 nb[2 * t + half, ROWS:] = gains[:, lanes]
         st["mean"], st["inv_std"] = mean, inv_std
 
-    st = {}
-
     def cot_start():
         cot_d.extend(gather_start(cg, S_COT))
 
@@ -340,47 +347,50 @@
     a_first()
     cot_start()
     tiles_sort()
+    tiles_first()
     b_step(1)
+    a_step(0)
     relay_step(0)
     tiles_second()
-    tiles_z(8,7,9,6,10)
+    tiles_z(1,15,2,14)
     b_step(2)
-    tiles_z(5,11,4,12,3)
+    a_step(1)
+    tiles_z(3,13,4,12)
     relay_step(1)
-    a_step(0)
     b_step(3)
-    tiles_z(13,2,14,1,15)
+    a_step(2)
+    tiles_z(5,11,6,10)
     relay_step(2)
-    a_step(1)
     b_step(4)
+    a_step(3)
+    tiles_z(7,9,8)
     cot_pass()
     relay_step(3)
-    a_step(2)
     b_step(5)
+    a_step(4)
     relay_step(4)
-    a_step(3)
     tiles_last()
+    b_step(6)
+    a_step(5)
     tiles_after()
-    b_step(6)
+    tiles_order()
     relay_step(5)
-    a_step(4)
     b_step(7)
+    a_step(6)
     grads_ready()
     relay_step(6)
-    a_step(5)
     x_pass()
     b_step(8)
+    a_step(7)
+    relay_step(7)
     norm()
-    relay_step(7)
-    a_step(6)
+    relay_step(8)
+    a_step(8)
     project_qkv(0)
     project_qkv(1)
-    relay_step(8)
     project_qkv(2)
-    a_step(7)
     project_qkv(3)
     project_qkv(4)
-    a_step(8)
     project_qkv(5)
     project_qkv(6)
     for j in range(9):
@@ -432,6 +442,8 @@
             p = dot(grads[0], wbuf[0, rows], NT)
             p = p + dot(grads[1], wbuf[1, rows], NT) + dot(grads[2], wbuf[2, rows], NT)
             part_n[t % 2, n, t // 2] = p.astype(BF16)
+        if n == 0:
+            row_sums()
         sib_nd.append(copy(part_n.at[oc, n], sib_n.at[n], S_NS + n, (dp, tens(0, oc))))
 
     def fold(n):
@@ -460,12 +472,14 @@
         s1r = jnp.sum(jnp.where(eye, jnp.concatenate(s1, axis=0), 0.0), axis=0, keepdims=True)
         s2r = jnp.sum(jnp.where(eye, jnp.concatenate(s2, axis=0), 0.0), axis=0, keepdims=True)
         scal[tn] = jnp.concatenate([s1r, s2r, jnp.zeros((6, ROWS), F32)], axis=0)
+
+    def send_sums():
         own_s = scal.at[tn]
         sc_d.extend([copy(own_s, own_s, S_SC + k - 1, (dp, tens(k, c))) for k in (1, 2, 3)])
         sc_d.extend([copy(own_s, own_s, S_SC + 3 + k, (dp, tens(k, oc))) for k in range(4)])
 
     partial(0)
-    row_sums()
+    send_sums()
     partial(1)
     fold(0)
     partial(2)

time: 139 us -> 136 us (0.978)
    pallas_call x1, Pallas kernels: 133 us -> 132 us  [per_device(): pl.pallas_call(block_kernel, out_shape=[jax.ShapeDtypeStruct((ROWS, W), B...]
where the time goes in v4:
time: 136 us; the launch traced here: 135 us
  Pallas kernels  132 us (97%)
  local copies, waits for them, and re-layouts  2.34 us (2%)
    pallas_call x1, Pallas kernels, per_device(): pl.pallas_call(block_kernel, out_shape=[jax.ShapeDtypeStruct((ROWS, W), B...  132 us

profile of v4, /device:TPU:1, one launch (start us, length us, event | category | flops | bytes accessed | tf_op | source)
XLA Modules:
  0.0 134.7 jit_solution(14540112708033361741)
XLA Ops:
  0.6 131.7 %attention_block.1 = (bf16[256,384]{1,0:T(8,128)(2,1)}, bf16[256,384]{1,0:T(8,128)(2,1)}) custom-call(s32[1,32]{1,0:T(1,128)} %bitcast.14, s32[1,32]{1,0:T(1,128)} %bitcast.15, bf16[256,384]{1,0:T(8,128)(2,1)} %bitcast.8, bf16[256,384]{1,0:T(8,128)(2,1)} %bitcast.9, f32[8,1,384]{2,1,0:T(1,128)} %bitcast.13, bf16[3,48,384]{2,1,0:T(8,128)(2,1)} %wqkv_hbm.1, ...), custom_call_target="tpu_custom_call" | custom-call | tf_op jit(solution)/shard_map/attention_block/pallas_call | solution.py:578
  132.3 0.0 copy-start
  132.3 1.7 %copy.11 = bf16[32,8,384]{2,1,0:T(8,128)(2,1)} copy(bf16[32,8,384]{2,1,0:T(8,128)(2,1)} %bitcast.11) | data formatting | bytes 393216
  134.0 0.0 copy-done
  134.0 0.7 copy.12
Async XLA Ops:
  132.3 1.7 %copy-start = (bf16[256,384]{1,0:T(8,128)(2,1)S(1)}, bf16[256,384]{1,0:T(8,128)(2,1)}, u32[]{:S(2)}) copy-start(bf16[256,384]{1,0:T(8,128)(2,1)} %get-tuple-element.5) | copy-start | bytes 589828

commit v5 on v4

--- a/solution.py
+++ b/solution.py
@@ -351,10 +351,10 @@
     b_step(1)
     a_step(0)
     relay_step(0)
+    b_step(2)
+    a_step(1)
     tiles_second()
     tiles_z(1,15,2,14)
-    b_step(2)
-    a_step(1)
     tiles_z(3,13,4,12)
     relay_step(1)
     b_step(3)
@@ -577,7 +577,7 @@
     ]
     mixed, grad = pl.pallas_call(
         block_kernel,
-        out_shape=[jax.ShapeDtypeStruct((ROWS, W), BF16)] * 2,
+        out_shape=[pltpu.VMEM((ROWS, W), BF16)] * 2,
         in_specs=[vm] * 2 + [pl.BlockSpec(memory_space=pl.ANY)] * 5,
         out_specs=[vm] * 2,
         scratch_shapes=scratch,

time: 136 us -> 134 us (0.985)
  no operation moved by 1% of the time
where the time goes in v5:
time: 134 us; the launch traced here: 133 us
  Pallas kernels  131 us (98%)
  local copies, waits for them, and re-layouts  1.36 us (1%)
    pallas_call x1, Pallas kernels, per_device(): pl.pallas_call(block_kernel, out_shape=[pltpu.VMEM((ROWS, W), BF16)] * 2,...  131 us

profile of v5, /device:TPU:1, one launch (start us, length us, event | category | flops | bytes accessed | tf_op | source)
XLA Modules:
  0.0 133.1 jit_solution(16934115807670986475)
XLA Ops:
  0.6 131.1 %attention_block.1 = (bf16[256,384]{1,0:T(8,128)(2,1)S(1)}, bf16[256,384]{1,0:T(8,128)(2,1)S(1)}) custom-call(s32[1,32]{1,0:T(1,128)} %bitcast.14, s32[1,32]{1,0:T(1,128)} %bitcast.15, bf16[256,384]{1,0:T(8,128)(2,1)} %bitcast.10, bf16[256,384]{1,0:T(8,128)(2,1)} %bitcast.11, f32[8,1,384]{2,1,0:T(1,128)} %bitcast.13, bf16[3,48,384]{2,1,0:T(8,128)(2,1)} %wqkv_hbm.1, ...), custom_call_target="tpu_custom_call" | custom-call | tf_op jit(solution)/shard_map/attention_block/pallas_call | solution.py:578
  131.8 0.7 copy.11
  132.4 0.7 copy.12

commit v6 on v5

--- a/solution.py
+++ b/solution.py
@@ -383,9 +383,12 @@
     b_step(8)
     a_step(7)
     relay_step(7)
+    for j in range(8):
+        project_grad(j)
     norm()
     relay_step(8)
     a_step(8)
+    project_grad(8)
     project_qkv(0)
     project_qkv(1)
     project_qkv(2)
@@ -393,8 +396,6 @@
     project_qkv(4)
     project_qkv(5)
     project_qkv(6)
-    for j in range(9):
-        project_grad(j)
     project_qkv(7)
     project_qkv(8)
     live, live_row, mean, inv_std = st["live"], st["live_row"], st["mean"], st["inv_std"]

time: 134 us -> 135 us (level)
  Pallas kernels: 131 us -> 133 us
    pallas_call x1, Pallas kernels: 131 us -> 133 us  [per_device(): pl.pallas_call(block_kernel, out_shape=[pltpu.VMEM((ROWS, W), BF16)] * 2,...]
where the time goes in v6:
time: 135 us
  Pallas kernels  133 us (99%)
  local copies, waits for them, and re-layouts  1.36 us (1%)
    pallas_call x1, Pallas kernels, per_device(): pl.pallas_call(block_kernel, out_shape=[pltpu.VMEM((ROWS, W), BF16)] * 2,...  133 us

profile of v6, /device:TPU:1, one launch (start us, length us, event | category | flops | bytes accessed | tf_op | source)
XLA Modules:
  0.0 134.6 jit_solution(5508325864103535715)
XLA Ops:
  0.6 132.6 %attention_block.1 = (bf16[256,384]{1,0:T(8,128)(2,1)S(1)}, bf16[256,384]{1,0:T(8,128)(2,1)S(1)}) custom-call(s32[1,32]{1,0:T(1,128)} %bitcast.14, s32[1,32]{1,0:T(1,128)} %bitcast.15, bf16[256,384]{1,0:T(8,128)(2,1)} %bitcast.10, bf16[256,384]{1,0:T(8,128)(2,1)} %bitcast.11, f32[8,1,384]{2,1,0:T(1,128)} %bitcast.13, bf16[3,48,384]{2,1,0:T(8,128)(2,1)} %wqkv_hbm.1, ...), custom_call_target="tpu_custom_call" | custom-call | tf_op jit(solution)/shard_map/attention_block/pallas_call | solution.py:579
  133.2 0.7 copy.11
  133.9 0.7 copy.12
